TPU v7x, 128 devices: a whole 4x4x4 slice. The times are simulated.
128 devices in a mesh: fsdp: 16 (over x, y), tp: 8 (over z, core).
Axes of the slice: x: 4, y: 4, z: 4, core: 2. Of those that a mesh axis runs over, the one named last changes fastest.
Arguments:
- grad: bfloat16 [4096, 16384], P('fsdp', 'tp'), may hold values from -34 to 34
- left_stat: float32 [8192, 8192], P('fsdp', 'tp'), may hold values from -0.75 to 3.2
- right_stat: float32 [8192, 8192], P('fsdp', 'tp'), may hold values from -0.75 to 3.2
- left_root: bfloat16 [8192, 8192], P('fsdp', 'tp'), may hold values from -0.65 to 2.2
- right_root: bfloat16 [8192, 8192], P('fsdp', 'tp'), may hold values from -0.65 to 2.2
- block_slot: int32 [8, 8], P('tp'), may hold values from 0 to 7, each once within a row
Outputs:
- new_left: float32 [8192, 8192], P('fsdp', 'tp')
- new_right: float32 [8192, 8192], P('fsdp', 'tp')
- update: bfloat16 [4096, 16384], P('fsdp', 'tp')
- grad_rms: float32 [], replicated
Inputs may be any that keep to these rules, and one draw needn't show every extreme that they name: `block_slot`: row t names each slot of column group t once; each slot's matrix S of left_stat, right_stat, left_root and right_root is symmetric.
All inputs are finite; a program needn't handle non-finite values.
Results may differ from a plain program's by a relative error of at most 0.0058.
Values may be sent and summed in bfloat16 or wider, within the bound.
No kernel may reach another device: no remote copies, remote signals or barrier semaphores. Data moves between devices by JAX's collectives and lax.ppermute only.
A program may use at most 128 MiB of HBM per device.

v0:
```python
import jax
import jax.numpy as jnp
from jax import lax
from jax.sharding import PartitionSpec as P

ROWS = 4096
COLS = 16384
BLOCK = 1024
HALF_BLOCK = 512


ema_decay = 0.9
clip_level = 0.0625
norm_eps = 1e-06


def swapped(value, axis, bit):
    mask = 2**bit
    pairs = [(source, source ^ mask) for source in range(lax.axis_size(axis))]
    return lax.ppermute(value, axis, pairs)


def join_halves(own_half, other_half, pair_side):
    upper_half = jnp.where(pair_side == 0, own_half, other_half)
    lower_half = jnp.where(pair_side == 0, other_half, own_half)
    return jnp.concatenate([upper_half, lower_half], axis=0)


def place_rows(halves, row_base, col_base, count, cols_dev):
    padded = jnp.pad(halves[0], ((count, count), (0, 0)))
    first_row = jnp.clip(count - row_base[0], 0, HALF_BLOCK + count)
    window = lax.dynamic_slice_in_dim(padded, first_row, count, 0).astype(jnp.float32)
    placed = lax.dynamic_update_slice_in_dim(
        jnp.zeros((count, cols_dev), jnp.float32), window, col_base[0], 1
    )
    return placed


def per_device(grad, left_stat, right_stat, left_root, right_root, block_slot):
    rows_dev, cols_dev = grad.shape
    col_blocks = cols_dev // BLOCK
    slots_pair = left_stat.shape[0] // HALF_BLOCK
    col_slots = block_slot.shape[1]
    fsdp_index = lax.axis_index("fsdp")
    pair_index = fsdp_index // 2
    pair_side = fsdp_index % 2
    slot_table = block_slot[0]
    slot_ids = jnp.arange(col_slots, dtype=jnp.int32)
    holder = jnp.sum(
        jnp.where(slot_table[None, :] == slot_ids[:, None], slot_ids[None, :], 0), axis=1
    )
    owned_blocks = lax.dynamic_slice_in_dim(holder, pair_index * slots_pair, slots_pair)
    block_row = owned_blocks // col_blocks
    block_col = owned_blocks % col_blocks
    local_sum = jnp.sum(jnp.square(grad.astype(jnp.float32)))
    sum_squares = lax.psum(local_sum, ("fsdp", "tp"))
    grad_rms = jnp.sqrt(sum_squares / (ROWS * COLS) + norm_eps)
    factor = jnp.minimum(1.0, clip_level / grad_rms)
    clipped = (grad.astype(jnp.float32) * factor).astype(jnp.bfloat16)
    column = lax.all_gather(clipped, "fsdp", axis=0, tiled=True)
    blocks = [
        lax.dynamic_slice(column, (block_row[0] * BLOCK, block_col[0] * BLOCK), (BLOCK, BLOCK))
    ]
    position = 0
    current = blocks[position]
    rows_half = lax.dynamic_slice_in_dim(current, pair_side * HALF_BLOCK, HALF_BLOCK, 0)
    cols_half = lax.dynamic_slice_in_dim(current, pair_side * HALF_BLOCK, HALF_BLOCK, 1)
    gram_left = jnp.dot(rows_half, current.T, preferred_element_type=jnp.float32)
    gram_right = lax.dot_general(
        cols_half, current, (((0,), (0,)), ((), ())), preferred_element_type=jnp.float32
    )
    left_parts = ema_decay * left_stat + (1.0 - ema_decay) * gram_left
    right_parts = ema_decay * right_stat + (1.0 - ema_decay) * gram_right
    other_left, other_right = swapped((left_root, right_root), "fsdp", 0)
    position = 0
    left_full = join_halves(left_root, other_left, pair_side)
    right_full = join_halves(right_root, other_right, pair_side)
    partial_value = jnp.dot(left_full, blocks[position], preferred_element_type=jnp.float32).astype(
        jnp.bfloat16
    )
    product = jnp.dot(partial_value, right_full, preferred_element_type=jnp.float32).astype(
        jnp.bfloat16
    )
    results = [lax.dynamic_slice_in_dim(product, pair_side * HALF_BLOCK, HALF_BLOCK, 0)]
    halves = jnp.stack(results)
    row_base = block_row * BLOCK + pair_side * HALF_BLOCK
    col_base = block_col * BLOCK
    update = lax.psum_scatter(
        place_rows(halves, row_base, col_base, rows_dev * lax.axis_size("fsdp"), cols_dev).astype(
            jnp.bfloat16
        ),
        "fsdp",
        scatter_dimension=0,
        tiled=True,
    )
    return (left_parts, right_parts, update, grad_rms)


def solution(mesh):
    in_specs = (
        P("fsdp", "tp"),
        P("fsdp", "tp"),
        P("fsdp", "tp"),
        P("fsdp", "tp"),
        P("fsdp", "tp"),
        P("tp", None),
    )
    out_specs = (P("fsdp", "tp"), P("fsdp", "tp"), P("fsdp", "tp"), P())
    return jax.shard_map(
        per_device, mesh=mesh, in_specs=in_specs, out_specs=out_specs, check_vma=False
    )
```

profile of v0, /device:TPU:0, one launch (start us, length us, event | category | flops | bytes accessed | tf_op | source)
XLA Modules:
  0.0 354.5 jit_solution(7733626664331344714)
XLA Ops:
  7.2 0.0 all-gather.2.cloned.1.call-start
  7.2 2.5 fusion
  9.7 68.2 %psum.7 = f32[]{:T(128)} all-reduce(f32[]{:T(128)} %fusion), channel_id=1, replica_groups=mesh['fsdp'=16,'tp'=8] {'fsdp','tp'}, use_global_device_ids=true, to_apply=%region_1.2 | all-reduce | flops 1 | bytes 8 | tf_op jit(solution)/shard_map/psum | solution.py:56
  78.7 2.4 fusion.1
  81.1 0.0 all-gather.2.cloned.1.call-update
  81.1 0.0 reduce-scatter.2.cloned.1.call-start
  81.2 0.3 collective-permute-start
  81.4 1.8 collective-permute-start.1
  83.3 0.1 select_reduce_fusion
  83.4 0.6 dynamic_slice.22
  86.6 36.7 %collective-permute-done = bf16[512,1024]{1,0:T(8,128)(2,1)} collective-permute-done((bf16[512,1024]{1,0:T(8,128)(2,1)S(1)}, bf16[512,1024]{1,0:T(8,128)(2,1)}, u32[]{:S(2)}, u32[]{:S(2)}) %collective-permute-start) | collective-permute-done | bytes 1048608 | tf_op jit(solution)/shard_map/ppermute | solution.py:20
  123.4 2.7 broadcast_select_fusion.3
  126.1 29.2 %collective-permute-done.1 = bf16[512,1024]{1,0:T(8,128)(2,1)S(1)} collective-permute-done((bf16[512,1024]{1,0:T(8,128)(2,1)S(1)}, bf16[512,1024]{1,0:T(8,128)(2,1)S(1)}, u32[]{:S(2)}, u32[]{:S(2)}) %collective-permute-start.1) | collective-permute-done | bytes 1048608 | tf_op jit(solution)/shard_map/ppermute | solution.py:20
  155.3 1.5 broadcast_select_fusion.1
  156.8 56.4 %all-gather.2.cloned.1.call-done = bf16[4096,2048]{1,0:T(8,128)(2,1)} async-done(((bf16[256,2048]{1,0:T(8,128)(2,1)}), bf16[4096,2048]{1,0:T(8,128)(2,1)}) %all-gather.2.cloned.1.call-update) | async-done | bytes 16777232 | tf_op jit(solution)/shard_map/all_gather | solution.py:60
  213.1 8.3 %fusion.6 = bf16[1024,1024]{1,0:T(8,128)(2,1)} fusion(bf16[512,1024]{1,0:T(8,128)(2,1)} %get-tuple-element.7, bf16[512,1024]{1,0:T(8,128)(2,1)} %get-tuple-element.6, bf16[512,1024]{1,0:T(8,128)(2,1)} %get-tuple-element.5, bf16[512,1024]{1,0:T(8,128)(2,1)S(1)} %copy-done.2, bf16[4096,2048]{1,0:T(8,128)(2,1)} %all-gather.2.cloned.1.call-done, ...), kind=kOutput, calls=%fused_computation.11 | convolution fusion | flops 4304404480 | bytes 8388616 | tf_op jit(solution)/shard_map/dot_general | solution.py:81
  221.4 1.3 dynamic-slice_convert_fusion
  222.7 6.2 %broadcast_in_dim.19 = bf16[4096,2048]{1,0:T(8,128)(2,1)} broadcast(bf16[]{:T(256)} %constant.140), dimensions={} | broadcast | bytes 16777218 | tf_op jit(solution)/shard_map/broadcast_in_dim | solution.py:34
  228.9 10.5 %convert_dynamic-update-slice_fusion = bf16[4096,2048]{1,0:T(8,128)(2,1)} fusion(bf16[4096,2048]{1,0:T(8,128)(2,1)} %broadcast_in_dim.19, s32[]{:T(128)S(6)} %select_n.78, s32[]{:T(128)} %bitcast.4, bf16[512,1024]{1,0:T(8,128)(2,1)S(1)} %dynamic-slice_convert_fusion), kind=kLoop, calls=%fused_computation.1 | loop fusion | flops 4194304 | bytes 17826308 | tf_op jit(solution)/shard_map/dynamic_update_slice | solution.py:33
  239.4 0.0 reduce-scatter.2.cloned.1.call-update
  239.5 1.5 copy-done.3
  241.0 4.9 %multiply_add_fusion = f32[512,1024]{1,0:T(8,128)} fusion(f32[512,1024]{1,0:T(8,128)S(1)} %copy-done.3, bf16[4096,2048]{1,0:T(8,128)(2,1)} %all-gather.2.cloned.1.call-done, s32[]{:T(128)S(6)} %select_n.75, s32[]{:T(128)S(6)} %select_n.78, s32[]{:T(128)S(6)} %select_n.76, s32[]{:T(128)S(6)} %dynamic_slice.26), kind=kOutput, calls=%fused_computation.16 | convolution fusion | flops 1075314688 | bytes 7340048 | tf_op jit(solution)/shard_map/dot_general | solution.py:69
  246.0 4.7 %multiply_add_fusion.1 = f32[512,1024]{1,0:T(8,128)} fusion(f32[512,1024]{1,0:T(8,128)S(1)} %copy-done.4, bf16[4096,2048]{1,0:T(8,128)(2,1)} %all-gather.2.cloned.1.call-done, s32[]{:T(128)S(6)} %select_n.75, s32[]{:T(128)S(6)} %select_n.78, s32[]{:T(128)S(6)} %dynamic_slice.23, s32[]{:T(128)S(6)} %select_n.79), kind=kOutput, calls=%fused_computation.17 | convolution fusion | flops 1075314688 | bytes 7340048 | tf_op jit(solution)/shard_map/dot_general | solution.py:68
  250.6 95.9 %reduce-scatter.2.cloned.1.call-done = bf16[256,2048]{1,0:T(8,128)(2,1)} async-done(((bf16[4096,2048]{1,0:T(8,128)(2,1)}), bf16[256,2048]{1,0:T(8,128)(2,1)}) %reduce-scatter.2.cloned.1.call-update) | async-done | bytes 1048592 | tf_op jit(solution)/shard_map/reduce_scatter | solution.py:88
  (11 shorter events, 0.0 us)
Async XLA Ops:
  7.2 74.0 %copy-start = (bf16[512,1024]{1,0:T(8,128)(2,1)S(1)}, bf16[512,1024]{1,0:T(8,128)(2,1)}, u32[]{:S(2)}) copy-start(bf16[512,1024]{1,0:T(8,128)(2,1)} %param.9) | copy-start | bytes 3145732
  7.2 74.3 %copy-start.1 = (bf16[512,1024]{1,0:T(8,128)(2,1)S(1)}, bf16[512,1024]{1,0:T(8,128)(2,1)}, u32[]{:S(2)}) copy-start(bf16[512,1024]{1,0:T(8,128)(2,1)} %param.10) | copy-start | bytes 3145732
  7.2 76.1 %copy-start.5 = (s32[1,8]{1,0:T(1,128)S(1)}, s32[1,8]{1,0:T(1,128)}, u32[]{:S(2)}) copy-start(s32[1,8]{1,0:T(1,128)} %param.11) | copy-start | bytes 100
  7.2 205.9 %all-gather.2.cloned.1.call-start = ((), (), s32[]{:S(2)}) async-start(), calls=%async_computation.1 | async-start | bytes 17825792 | tf_op jit(solution)/shard_map/all_gather | solution.py:60
  81.1 265.4 %reduce-scatter.2.cloned.1.call-start = ((), (), s32[]{:S(2)}) async-start(), calls=%async_computation.2 | async-start | bytes 17825792 | tf_op jit(solution)/shard_map/reduce_scatter | solution.py:88
  81.2 42.2 %collective-permute-start = (bf16[512,1024]{1,0:T(8,128)(2,1)S(1)}, bf16[512,1024]{1,0:T(8,128)(2,1)}, u32[]{:S(2)}, u32[]{:S(2)}) collective-permute-start(bf16[512,1024]{1,0:T(8,128)(2,1)S(1)} %copy-done), channel_id=1, source_target_pairs={{0,8},{8,0},{16,24},{24,16},{32,40},{40,32},{48,56},{56,48},{64,72... | collective-permute-start | bytes 3145736 | tf_op jit(solution)/shard_map/ppermute | solution.py:20
  81.4 73.9 %collective-permute-start.1 = (bf16[512,1024]{1,0:T(8,128)(2,1)S(1)}, bf16[512,1024]{1,0:T(8,128)(2,1)S(1)}, u32[]{:S(2)}, u32[]{:S(2)}) collective-permute-start(bf16[512,1024]{1,0:T(8,128)(2,1)S(1)} %copy-done.1), channel_id=1, source_target_pairs={{0,8},{8,0},{16,24},{24,16},{32,40},{40,32},{48,56},{56,48},{64,72... | collective-permute-start | bytes 3145736 | tf_op jit(solution)/shard_map/ppermute | solution.py:20
  126.1 87.1 %copy-start.2 = (bf16[512,1024]{1,0:T(8,128)(2,1)S(1)}, bf16[512,1024]{1,0:T(8,128)(2,1)}, u32[]{:S(2)}) copy-start(bf16[512,1024]{1,0:T(8,128)(2,1)} %get-tuple-element.4) | copy-start | bytes 3145732
  239.4 1.6 copy-start.3
  241.0 4.9 %copy-start.4 = (f32[512,1024]{1,0:T(8,128)S(1)}, f32[512,1024]{1,0:T(8,128)}, u32[]{:S(2)}) copy-start(f32[512,1024]{1,0:T(8,128)} %param.7) | copy-start | bytes 6291460
Sparse Core Ops, SparseCore 0:
  81.2 131.8 all-gather.1
  239.6 106.9 reduce-scatter.1
where the time goes:
time: 355 us
  waiting for transfers between devices  218 us (61%)
  blocking collectives  68.2 us (19%)
  other arithmetic  19.7 us (6%)
  between operations  18.6 us (5%)
  matrix products  17.9 us (5%)
  local copies, waits for them, and re-layouts  9.6 us (3%)
    reduce_scatter x1, waiting for transfers between devices, per_device(): lax.psum_scatter(place_rows(halves, row_base, col_base, rows_dev * lax.ax...  95.9 us
    psum x1, blocking collectives, per_device(): sum_squares = lax.psum(local_sum, ('fsdp', 'tp'))  68.2 us
    ppermute x2, waiting for transfers between devices, swapped(): return lax.ppermute(value, axis, pairs)  66 us
    all_gather x1, waiting for transfers between devices, per_device(): column = lax.all_gather(clipped, 'fsdp', axis=0, tiled=True)  56.4 us
    dynamic_update_slice x1, other arithmetic, place_rows(): lax.dynamic_update_slice_in_dim(jnp.zeros((count, cols_dev), jnp.float32)...  10.5 us
    dot_general x1, matrix products, per_device(): jnp.dot(partial_value, right_full, preferred_element_type=jnp.float32)  8.31 us
  transfers between devices with their start and end apart: 4, of which 4 were waited for; matrix products, arithmetic and copies ran while one was open for 4% of the time, Pallas kernels for 0%

commit v1 on v0

v1 whole, which is shorter than its diff:
```python
import jax
import jax.numpy as jnp
from jax import lax
from jax.experimental import pallas as pl
from jax.experimental.pallas import tpu as pltpu
from jax.sharding import Mesh, PartitionSpec as P

ROWS = 4096
COLS = 16384
BLOCK = 1024
HALF = 512
NX = 4
NY = 4
PIECE = BLOCK // (NX * NY)


ema_decay = 0.9
clip_level = 0.0625
norm_eps = 1e-06

FSDP = ("x", "y")
VMEM = pl.BlockSpec(memory_space=pltpu.VMEM)
SMEM = pl.BlockSpec(memory_space=pltpu.SMEM)


def sum_over_all(value):
    for axis, bits in (("x", 2), ("y", 2), ("tp", 3)):
        for bit in range(bits):
            size = 2**bits
            pairs = [(source, source ^ (1 << bit)) for source in range(size)]
            value = value + lax.ppermute(value, axis, pairs)
    return value


def to_keepers_kernel(slot_ref, src_ref, dst_ref):
    for j in range(8):
        slot = slot_ref[0, j]
        x = slot // 2
        y = (slot % 2) * 2
        piece = src_ref[j // 2, :, (j % 2) * BLOCK : (j % 2 + 1) * BLOCK]
        dst_ref[y * NX + x] = piece
        dst_ref[(y + 1) * NX + x] = piece


def to_rows_kernel(slot_ref, src_ref, dst_ref):
    for j in range(8):
        slot = slot_ref[0, j]
        x = slot // 2
        y = (slot % 2) * 2
        for half in range(2):
            start = (j % 2) * BLOCK + half * HALF
            dst_ref[j // 2, :, start : start + HALF] = src_ref[(y + half) * NX + x]


def update_kernel(side_ref, factor_ref, g_ref, own_left_ref, other_left_ref, right_ref, out_ref, t_ref):
    tile = 256
    for i in range(BLOCK // tile):
        rows = slice(i * tile, (i + 1) * tile)
        t_ref[rows, :] = lax.dot_general(
            g_ref[rows, :], right_ref[...], (((1,), (1,)), ((), ())), preferred_element_type=jnp.float32
        ).astype(jnp.bfloat16)
    factor = factor_ref[0]
    per_tile = tile // PIECE
    for part, left_ref in ((0, own_left_ref), (1, other_left_ref)):
        base = (side_ref[0] ^ part) * (HALF // PIECE)
        for i in range(HALF // tile):
            rows = slice(i * tile, (i + 1) * tile)
            product = jnp.dot(left_ref[rows, :], t_ref[...], preferred_element_type=jnp.float32)
            product = (product * factor).astype(jnp.bfloat16)
            out_ref[pl.ds(base + i * per_tile, per_tile)] = product.reshape(per_tile, PIECE, HALF)


def per_device(grad, left_stat, right_stat, left_root, right_root, block_slot):
    side = lax.axis_index("y") % 2
    other_left = lax.ppermute(left_root, "y", [(i, i ^ 1) for i in range(NY)])
    local_sum = jnp.sum(jnp.square(grad.astype(jnp.float32)))
    sum_squares = sum_over_all(local_sum.reshape(1, 1))[0, 0]
    grad_rms = jnp.sqrt(sum_squares / (ROWS * COLS) + norm_eps)
    factor = jnp.minimum(1.0, clip_level / grad_rms)

    spread = lax.all_to_all(grad.reshape(NX, NX * PIECE // NX, 2 * BLOCK), "x", 0, 0)
    send = pl.pallas_call(
        to_keepers_kernel,
        out_shape=jax.ShapeDtypeStruct((NX * NY, PIECE, BLOCK), jnp.bfloat16),
        in_specs=[SMEM, VMEM],
        out_specs=VMEM,
    )(block_slot, spread)
    g = lax.all_to_all(send, ("y", "x"), 0, 0).reshape(BLOCK, BLOCK)

    out = pl.pallas_call(
        update_kernel,
        out_shape=jax.ShapeDtypeStruct((NX * NY, PIECE, HALF), jnp.bfloat16),
        in_specs=[SMEM, SMEM, VMEM, VMEM, VMEM, VMEM],
        out_specs=VMEM,
        scratch_shapes=[pltpu.VMEM((BLOCK, HALF), jnp.bfloat16)],
        compiler_params=pltpu.CompilerParams(vmem_limit_bytes=32 * 1024 * 1024),
    )(side.reshape(1), factor.reshape(1), g, left_root, other_left, right_root)
    back = lax.all_to_all(out, ("y", "x"), 0, 0)
    rows = pl.pallas_call(
        to_rows_kernel,
        out_shape=jax.ShapeDtypeStruct((NX, PIECE, 2 * BLOCK), jnp.bfloat16),
        in_specs=[SMEM, VMEM],
        out_specs=VMEM,
    )(block_slot, back)
    update = lax.all_to_all(rows, "x", 0, 0).reshape(grad.shape)

    scale = (1.0 - ema_decay) * factor * factor
    rows_half = lax.dynamic_slice_in_dim(g, side * HALF, HALF, 0)
    cols_half = lax.dynamic_slice_in_dim(g, side * HALF, HALF, 1)
    gram_left = lax.dot_general(
        rows_half, g, (((1,), (1,)), ((), ())), preferred_element_type=jnp.float32
    )
    gram_right = lax.dot_general(
        cols_half, g, (((0,), (0,)), ((), ())), preferred_element_type=jnp.float32
    )
    new_left = ema_decay * left_stat + scale * gram_left
    new_right = ema_decay * right_stat + scale * gram_right
    return (new_left, new_right, update, grad_rms)


def solution(mesh):
    grid = Mesh(mesh.devices.reshape(NX, NY, mesh.shape["tp"]), ("x", "y", "tp"))
    split = P(FSDP, "tp")
    return jax.shard_map(
        per_device,
        mesh=grid,
        in_specs=(split, split, split, split, split, P("tp", None)),
        out_specs=(split, split, split, P()),
        check_vma=False,
    )
```

time: 355 us -> 144 us (0.41)
  waiting for transfers between devices: 218 us -> 46.7 us
  blocking collectives: 68.2 us -> 19.6 us
  starting transfers between devices: 2.18 us -> 47.5 us
  other arithmetic: 19.7 us -> 2.37 us
  between operations: 18.6 us -> 7.02 us
  matrix products: 17.9 us -> 6.98 us
  Pallas kernels: 0 us -> 9.55 us
  local copies, waits for them, and re-layouts: 9.6 us -> 3.17 us
    reduce_scatter x1 -> x0, waiting for transfers between devices: 95.9 us -> none  [per_device(): lax.psum_scatter(place_rows(halves, row_base, col_base, rows_dev * lax.ax...]
    psum x1 -> x0, blocking collectives: 68.2 us -> none  [per_device(): sum_squares = lax.psum(local_sum, ('fsdp', 'tp'))]
    all_gather x1 -> x0, waiting for transfers between devices: 56.4 us -> none  [per_device(): column = lax.all_gather(clipped, 'fsdp', axis=0, tiled=True)]
    ppermute x2 -> x8, waiting for transfers between devices: 66 us -> 25 us  [the longest x7 25 us: sum_over_all(): value = value + lax.ppermute(value, axis, pairs)]
    ppermute x2 -> x8, starting transfers between devices: 2.11 us -> 32 us  [the longest x7 30 us: sum_over_all(): value = value + lax.ppermute(value, axis, pairs)]
    all_to_all x0 -> x3, waiting for transfers between devices: none -> 21.7 us  [the longest x1 16.2 us: per_device(): back = lax.all_to_all(out, ('y', 'x'), 0, 0)]
    all_to_all x0 -> x1, blocking collectives: none -> 19.6 us  [per_device(): lax.all_to_all(grad.reshape(NX, NX * PIECE // NX, 2 * BLOCK), 'x', 0, 0)]
    all_to_all x0 -> x3, starting transfers between devices: none -> 15.5 us  [the longest x1 6.46 us: per_device(): back = lax.all_to_all(out, ('y', 'x'), 0, 0)]
  transfers between devices with their start and end apart: 4 -> 11, of which waited for: 4 -> 9; matrix products, arithmetic and copies ran while one was open for 4% -> 7% of each run, Pallas kernels for 0% -> 0%
where the time goes in v1:
time: 144 us; the launch traced here: 143 us
  starting transfers between devices  47.5 us (33%)
  waiting for transfers between devices  46.7 us (32%)
  blocking collectives  19.6 us (14%)
  Pallas kernels  9.55 us (7%)
  between operations  7.02 us (5%)
  matrix products  6.98 us (5%)
  local copies, waits for them, and re-layouts  3.17 us (2%)
  other arithmetic  2.37 us (2%)
    ppermute x7, starting transfers between devices, sum_over_all(): value = value + lax.ppermute(value, axis, pairs)  30 us
    ppermute x7, waiting for transfers between devices, sum_over_all(): value = value + lax.ppermute(value, axis, pairs)  25 us
    all_to_all x1, blocking collectives, per_device(): lax.all_to_all(grad.reshape(NX, NX * PIECE // NX, 2 * BLOCK), 'x', 0, 0)  19.6 us
    all_to_all x1, waiting for transfers between devices, per_device(): back = lax.all_to_all(out, ('y', 'x'), 0, 0)  16.2 us
    all_to_all x1, starting transfers between devices, per_device(): back = lax.all_to_all(out, ('y', 'x'), 0, 0)  6.46 us
    all_to_all x1, starting transfers between devices, per_device(): g = lax.all_to_all(send, ('y', 'x'), 0, 0).reshape(BLOCK, BLOCK)  5.49 us
    all_to_all x1, waiting for transfers between devices, per_device(): update = lax.all_to_all(rows, 'x', 0, 0).reshape(grad.shape)  5.48 us
    pallas_call x1, Pallas kernels, per_device(): pl.pallas_call(update_kernel, out_shape=jax.ShapeDtypeStruct((NX * NY, PI...  4.56 us
  transfers between devices with their start and end apart: 11, of which 9 were waited for; matrix products, arithmetic and copies ran while one was open for 7% of the time, Pallas kernels for 0%

profile of v1, /device:TPU:0, one launch (start us, length us, event | category | flops | bytes accessed | tf_op | source)
XLA Modules:
  0.0 142.9 jit_solution(8389138123531250209)
XLA Ops:
  0.6 19.6 %all_to_all.20.src_ref = bf16[4,64,2048]{2,1,0:T(8,128)(2,1)} all-to-all(bf16[4,64,2048]{2,1,0:T(8,128)(2,1)} %bitcast.12), channel_id=1, replica_groups=mesh['x'=4,'y'=4,'tp'=8] {'x'}, dimensions={0} | all-to-all | bytes 2097152 | tf_op jit(solution)/shard_map/all_to_all | solution.py:81
  20.2 2.7 %shard_map.93 = bf16[16,64,1024]{2,1,0:T(8,128)(2,1)} custom-call(s32[1,8]{1,0:T(1,128)} %slot_ref.3, bf16[4,64,2048]{2,1,0:T(8,128)(2,1)} %all_to_all.20.src_ref), custom_call_target="tpu_custom_call" | custom-call | tf_op jit(solution)/shard_map/pallas_call | solution.py:82
  22.9 5.5 %all-to-all-start.1 = ((bf16[16,64,1024]{2,1,0:T(8,128)(2,1)}), bf16[16,64,1024]{2,1,0:T(8,128)(2,1)S(1)}, u32[]{:S(2)}, u32[]{:S(2)}) async-start(bf16[16,64,1024]{2,1,0:T(8,128)(2,1)} %shard_map.93), calls=%async_computation.1 | async-start | bytes 4194304 | tf_op jit(solution)/shard_map/all_to_all | solution.py:88
  28.4 2.0 %collective-permute-start.7 = (bf16[512,1024]{1,0:T(8,128)(2,1)S(1)}, bf16[512,1024]{1,0:T(8,128)(2,1)}, u32[]{:S(2)}, u32[]{:S(2)}) collective-permute-start(bf16[512,1024]{1,0:T(8,128)(2,1)S(1)} %copy-done), channel_id=1, source_target_pairs={{0,8},{8,0},{16,24},{24,16},{1,9},{9,1},{17,25},{25,17},{2,10},{10... | collective-permute-start | bytes 3145736 | tf_op jit(solution)/shard_map/ppermute | solution.py:75
  30.4 2.4 %multiply_reduce_fusion = f32[]{:T(128)} fusion(bf16[256,2048]{1,0:T(8,128)(2,1)} %param.6), kind=kLoop, calls=%fused_computation.2 | loop fusion | flops 1572863 | bytes 1048580 | tf_op jit(solution)/shard_map/reduce_sum | solution.py:76
  32.8 1.5 %collective-permute-start = (f32[1,1]{1,0:T(1,128)}, f32[1,1]{1,0:T(1,128)}, u32[]{:S(2)}, u32[]{:S(2)}) collective-permute-start(f32[1,1]{1,0:T(1,128)} %bitcast), channel_id=1, source_target_pairs={{0,32},{32,0},{64,96},{96,64},{1,33},{33,1},{65,97},{97,65},{2,34}... | collective-permute-start | bytes 20 | tf_op jit(solution)/shard_map/ppermute | solution.py:31
  34.3 19.4 %collective-permute-done = f32[1,1]{1,0:T(1,128)} collective-permute-done((f32[1,1]{1,0:T(1,128)}, f32[1,1]{1,0:T(1,128)}, u32[]{:S(2)}, u32[]{:S(2)}) %collective-permute-start) | collective-permute-done | bytes 36 | tf_op jit(solution)/shard_map/ppermute | solution.py:31
  54.9 3.5 %collective-permute-start.1 = (f32[1,1]{1,0:T(1,128)}, f32[1,1]{1,0:T(1,128)}, u32[]{:S(2)}, u32[]{:S(2)}) collective-permute-start(f32[1,1]{1,0:T(1,128)} %add.39), channel_id=1, source_target_pairs={{0,64},{32,96},{64,0},{96,32},{1,65},{33,97},{65,1},{97,33},{2,66}... | collective-permute-start | bytes 20 | tf_op jit(solution)/shard_map/ppermute | solution.py:31
  58.4 1.6 %collective-permute-done.1 = f32[1,1]{1,0:T(1,128)} collective-permute-done((f32[1,1]{1,0:T(1,128)}, f32[1,1]{1,0:T(1,128)}, u32[]{:S(2)}, u32[]{:S(2)}) %collective-permute-start.1) | collective-permute-done | bytes 36 | tf_op jit(solution)/shard_map/ppermute | solution.py:31
  60.6 11.6 %collective-permute-start.2 = (f32[1,1]{1,0:T(1,128)}, f32[1,1]{1,0:T(1,128)}, u32[]{:S(2)}, u32[]{:S(2)}) collective-permute-start(f32[1,1]{1,0:T(1,128)} %add.40), channel_id=1, source_target_pairs={{0,8},{8,0},{16,24},{24,16},{1,9},{9,1},{17,25},{25,17},{2,10},{10... | collective-permute-start | bytes 20 | tf_op jit(solution)/shard_map/ppermute | solution.py:31
  72.2 2.3 %collective-permute-done.2 = f32[1,1]{1,0:T(1,128)} collective-permute-done((f32[1,1]{1,0:T(1,128)}, f32[1,1]{1,0:T(1,128)}, u32[]{:S(2)}, u32[]{:S(2)}) %collective-permute-start.2) | collective-permute-done | bytes 36 | tf_op jit(solution)/shard_map/ppermute | solution.py:31
  75.1 4.1 %collective-permute-start.3 = (f32[1,1]{1,0:T(1,128)}, f32[1,1]{1,0:T(1,128)}, u32[]{:S(2)}, u32[]{:S(2)}) collective-permute-start(f32[1,1]{1,0:T(1,128)} %add.41), channel_id=1, source_target_pairs={{0,16},{8,24},{16,0},{24,8},{1,17},{9,25},{17,1},{25,9},{2,18},{10... | collective-permute-start | bytes 20 | tf_op jit(solution)/shard_map/ppermute | solution.py:31
  79.2 1.0 collective-permute-done.3
  82.7 3.3 %collective-permute-start.5 = (f32[1,1]{1,0:T(1,128)}, f32[1,1]{1,0:T(1,128)}, u32[]{:S(2)}, u32[]{:S(2)}) collective-permute-start(f32[1,1]{1,0:T(1,128)} %add.43), channel_id=1, source_target_pairs={{0,2},{1,3},{2,0},{3,1},{4,6},{5,7},{6,4},{7,5},{8,10},{9,11},{10,... | collective-permute-start | bytes 20 | tf_op jit(solution)/shard_map/ppermute | solution.py:31
  86.9 5.3 %collective-permute-start.6 = (f32[1,1]{1,0:T(1,128)}, f32[1,1]{1,0:T(1,128)}, u32[]{:S(2)}, u32[]{:S(2)}) collective-permute-start(f32[1,1]{1,0:T(1,128)} %add.44), channel_id=1, source_target_pairs={{0,4},{1,5},{2,6},{3,7},{4,0},{5,1},{6,2},{7,3},{8,12},{9,13},{10,... | collective-permute-start | bytes 20 | tf_op jit(solution)/shard_map/ppermute | solution.py:31
  93.1 1.2 copy-done.1
  94.3 4.6 %shard_map.94 = bf16[16,64,512]{2,1,0:T(8,128)(2,1)} custom-call(s32[1]{0:T(128)} %bitcast.4.side_ref, f32[1]{0:T(128)} %bitcast.5.factor_ref, bf16[1024,1024]{1,0:T(8,128)(2,1)S(1)} %bitcast.9, bf16[512,1024]{1,0:T(8,128)(2,1)S(1)} %copy-done, bf16[512,1024]{1,0:T(8,128)(2,1)} %collective-permute-done.7.other_left_ref, bf16[512,1024]{1,0:T(8,128)(2,1)S(1)} %copy-done.1), custom_call_target="tpu_custom_call" | custom-call | tf_op jit(solution)/shard_map/pallas_call | solution.py:90
  98.8 6.5 %all-to-all-start.2 = ((bf16[16,64,512]{2,1,0:T(8,128)(2,1)}), bf16[16,64,512]{2,1,0:T(8,128)(2,1)S(1)}, u32[]{:S(2)}, u32[]{:S(2)}) async-start(bf16[16,64,512]{2,1,0:T(8,128)(2,1)} %shard_map.94), calls=%async_computation.2 | async-start | bytes 2097152 | tf_op jit(solution)/shard_map/all_to_all | solution.py:98
  105.3 16.2 %all-to-all-done.2.src_ref = bf16[16,64,512]{2,1,0:T(8,128)(2,1)S(1)} async-done(((bf16[16,64,512]{2,1,0:T(8,128)(2,1)}), bf16[16,64,512]{2,1,0:T(8,128)(2,1)S(1)}, u32[]{:S(2)}, u32[]{:S(2)}) %all-to-all-start.2) | async-done | bytes 1048608 | tf_op jit(solution)/shard_map/all_to_all | solution.py:98
  122.5 2.3 %shard_map.95 = bf16[4,64,2048]{2,1,0:T(8,128)(2,1)} custom-call(s32[1,8]{1,0:T(1,128)} %slot_ref.3, bf16[16,64,512]{2,1,0:T(8,128)(2,1)} %copy-done.2), custom_call_target="tpu_custom_call" | custom-call | tf_op jit(solution)/shard_map/pallas_call | solution.py:99
  124.8 3.5 %all-to-all-start.3 = ((bf16[4,64,2048]{2,1,0:T(8,128)(2,1)}), bf16[4,64,2048]{2,1,0:T(8,128)(2,1)S(1)}, u32[]{:S(2)}, u32[]{:S(2)}) async-start(bf16[4,64,2048]{2,1,0:T(8,128)(2,1)} %shard_map.95), calls=%async_computation.3 | async-start | bytes 2097152 | tf_op jit(solution)/shard_map/all_to_all | solution.py:105
  128.3 4.4 %multiply_add_fusion.1 = f32[512,1024]{1,0:T(8,128)} fusion(f32[512,1024]{1,0:T(8,128)} %param.7, bf16[1024,1024]{1,0:T(8,128)(2,1)S(1)} %bitcast.10, s32[]{:T(128)S(6)} %select_n.12, f32[]{:T(128)S(6)} %mul.24), kind=kOutput, calls=%fused_computation.1 | convolution fusion | flops 1075314688 | bytes 7340040 | tf_op jit(solution)/shard_map/dot_general | solution.py:110
  132.7 2.6 %multiply_add_fusion = f32[512,1024]{1,0:T(8,128)} fusion(f32[512,1024]{1,0:T(8,128)S(1)} %copy-done.3, bf16[1024,1024]{1,0:T(8,128)(2,1)S(1)} %bitcast.11, s32[]{:T(128)S(6)} %select_n.12, f32[]{:T(128)S(6)} %mul.24), kind=kOutput, calls=%fused_computation | convolution fusion | flops 1075314688 | bytes 7340040 | tf_op jit(solution)/shard_map/dot_general | solution.py:113
  135.3 5.5 %all-to-all-done.3 = bf16[4,64,2048]{2,1,0:T(8,128)(2,1)S(1)} async-done(((bf16[4,64,2048]{2,1,0:T(8,128)(2,1)}), bf16[4,64,2048]{2,1,0:T(8,128)(2,1)S(1)}, u32[]{:S(2)}, u32[]{:S(2)}) %all-to-all-start.3) | async-done | bytes 1048608 | tf_op jit(solution)/shard_map/all_to_all | solution.py:105
  (14 shorter events, 3.6 us)
Async XLA Ops:
  22.9 5.5 %copy-start = (bf16[512,1024]{1,0:T(8,128)(2,1)S(1)}, bf16[512,1024]{1,0:T(8,128)(2,1)}, u32[]{:S(2)}) copy-start(bf16[512,1024]{1,0:T(8,128)(2,1)} %own_left_ref.1) | copy-start | bytes 3145732
  22.9 70.1 %all-to-all-start.1 = ((bf16[16,64,1024]{2,1,0:T(8,128)(2,1)}), bf16[16,64,1024]{2,1,0:T(8,128)(2,1)S(1)}, u32[]{:S(2)}, u32[]{:S(2)}) async-start(bf16[16,64,1024]{2,1,0:T(8,128)(2,1)} %shard_map.93), calls=%async_computation.1 | async-start | bytes 4194304 | tf_op jit(solution)/shard_map/all_to_all | solution.py:88
  28.4 64.6 %collective-permute-start.7 = (bf16[512,1024]{1,0:T(8,128)(2,1)S(1)}, bf16[512,1024]{1,0:T(8,128)(2,1)}, u32[]{:S(2)}, u32[]{:S(2)}) collective-permute-start(bf16[512,1024]{1,0:T(8,128)(2,1)S(1)} %copy-done), channel_id=1, source_target_pairs={{0,8},{8,0},{16,24},{24,16},{1,9},{9,1},{17,25},{25,17},{2,10},{10... | collective-permute-start | bytes 3145736 | tf_op jit(solution)/shard_map/ppermute | solution.py:75
  32.8 20.8 %collective-permute-start = (f32[1,1]{1,0:T(1,128)}, f32[1,1]{1,0:T(1,128)}, u32[]{:S(2)}, u32[]{:S(2)}) collective-permute-start(f32[1,1]{1,0:T(1,128)} %bitcast), channel_id=1, source_target_pairs={{0,32},{32,0},{64,96},{96,64},{1,33},{33,1},{65,97},{97,65},{2,34}... | collective-permute-start | bytes 20 | tf_op jit(solution)/shard_map/ppermute | solution.py:31
  54.9 5.1 %collective-permute-start.1 = (f32[1,1]{1,0:T(1,128)}, f32[1,1]{1,0:T(1,128)}, u32[]{:S(2)}, u32[]{:S(2)}) collective-permute-start(f32[1,1]{1,0:T(1,128)} %add.39), channel_id=1, source_target_pairs={{0,64},{32,96},{64,0},{96,32},{1,65},{33,97},{65,1},{97,33},{2,66}... | collective-permute-start | bytes 20 | tf_op jit(solution)/shard_map/ppermute | solution.py:31
  60.6 13.9 %collective-permute-start.2 = (f32[1,1]{1,0:T(1,128)}, f32[1,1]{1,0:T(1,128)}, u32[]{:S(2)}, u32[]{:S(2)}) collective-permute-start(f32[1,1]{1,0:T(1,128)} %add.40), channel_id=1, source_target_pairs={{0,8},{8,0},{16,24},{24,16},{1,9},{9,1},{17,25},{25,17},{2,10},{10... | collective-permute-start | bytes 20 | tf_op jit(solution)/shard_map/ppermute | solution.py:31
  75.1 5.1 %collective-permute-start.3 = (f32[1,1]{1,0:T(1,128)}, f32[1,1]{1,0:T(1,128)}, u32[]{:S(2)}, u32[]{:S(2)}) collective-permute-start(f32[1,1]{1,0:T(1,128)} %add.41), channel_id=1, source_target_pairs={{0,16},{8,24},{16,0},{24,8},{1,17},{9,25},{17,1},{25,9},{2,18},{10... | collective-permute-start | bytes 20 | tf_op jit(solution)/shard_map/ppermute | solution.py:31
  80.8 1.2 collective-permute-start.4
  82.7 3.6 %collective-permute-start.5 = (f32[1,1]{1,0:T(1,128)}, f32[1,1]{1,0:T(1,128)}, u32[]{:S(2)}, u32[]{:S(2)}) collective-permute-start(f32[1,1]{1,0:T(1,128)} %add.43), channel_id=1, source_target_pairs={{0,2},{1,3},{2,0},{3,1},{4,6},{5,7},{6,4},{7,5},{8,10},{9,11},{10,... | collective-permute-start | bytes 20 | tf_op jit(solution)/shard_map/ppermute | solution.py:31
  86.9 5.4 %collective-permute-start.6 = (f32[1,1]{1,0:T(1,128)}, f32[1,1]{1,0:T(1,128)}, u32[]{:S(2)}, u32[]{:S(2)}) collective-permute-start(f32[1,1]{1,0:T(1,128)} %add.44), channel_id=1, source_target_pairs={{0,4},{1,5},{2,6},{3,7},{4,0},{5,1},{6,2},{7,3},{8,12},{9,13},{10,... | collective-permute-start | bytes 20 | tf_op jit(solution)/shard_map/ppermute | solution.py:31
  93.0 1.2 copy-start.1
  98.8 22.7 %all-to-all-start.2 = ((bf16[16,64,512]{2,1,0:T(8,128)(2,1)}), bf16[16,64,512]{2,1,0:T(8,128)(2,1)S(1)}, u32[]{:S(2)}, u32[]{:S(2)}) async-start(bf16[16,64,512]{2,1,0:T(8,128)(2,1)} %shard_map.94), calls=%async_computation.2 | async-start | bytes 2097152 | tf_op jit(solution)/shard_map/all_to_all | solution.py:98
  121.5 1.0 copy-start.2
  124.8 16.0 %all-to-all-start.3 = ((bf16[4,64,2048]{2,1,0:T(8,128)(2,1)}), bf16[4,64,2048]{2,1,0:T(8,128)(2,1)S(1)}, u32[]{:S(2)}, u32[]{:S(2)}) async-start(bf16[4,64,2048]{2,1,0:T(8,128)(2,1)} %shard_map.95), calls=%async_computation.3 | async-start | bytes 2097152 | tf_op jit(solution)/shard_map/all_to_all | solution.py:105
  128.3 4.4 %copy-start.3 = (f32[512,1024]{1,0:T(8,128)S(1)}, f32[512,1024]{1,0:T(8,128)}, u32[]{:S(2)}) copy-start(f32[512,1024]{1,0:T(8,128)} %param.8) | copy-start | bytes 6291460

commit v2 on v1

v2 whole, which is shorter than its diff:
```python
import jax
import jax.numpy as jnp
from jax import lax
from jax.experimental import pallas as pl
from jax.experimental.pallas import tpu as pltpu
from jax.sharding import Mesh, PartitionSpec as P

ROWS = 4096
COLS = 16384
BLOCK = 1024
HALF = 512
NX = 4
NY = 4
PIECE = BLOCK // (NX * NY)
PIECE_ROWS = PIECE * BLOCK // 128


ema_decay = 0.9
clip_level = 0.0625
norm_eps = 1e-06

FSDP = ("x", "y")
VMEM = pl.BlockSpec(memory_space=pltpu.VMEM)
ANY = pl.BlockSpec(memory_space=pl.ANY)
HBM = pl.BlockSpec(memory_space=pltpu.HBM)
SMEM = pl.BlockSpec(memory_space=pltpu.SMEM)


def add_partner(value, bit):
    return value + lax.ppermute(value, "tp", [(i, i ^ (1 << bit)) for i in range(8)])


def run_copies(pairs, sems):
    copies = [pltpu.make_async_copy(src, dst, sems.at[i]) for i, (src, dst) in enumerate(pairs)]
    for copy in copies:
        copy.start()
    for copy in copies:
        copy.wait()


def to_keepers_kernel(slot_ref, sum_ref, src_ref, dst_ref):
    total = jnp.broadcast_to(sum_ref[...], (16, 128))
    high = total.astype(jnp.bfloat16).astype(jnp.float32)
    middle = (total - high).astype(jnp.bfloat16).astype(jnp.float32)
    low = total - high - middle
    row = lax.broadcasted_iota(jnp.int32, (16, 128), 0)
    terms = jnp.where(row == 0, high, jnp.where(row == 1, middle, low)).astype(jnp.bfloat16)
    for keeper in range(NX * NY):
        dst_ref[keeper, PIECE_ROWS : PIECE_ROWS + 16, :] = terms
    for j in range(8):
        slot = slot_ref[0, j]
        keeper = (slot % 2) * 2 * NX + slot // 2
        for chunk in range(8):
            start = (j % 2) * BLOCK + chunk * 128
            part = src_ref[j // 2, :, start : start + 128]
            rows = slice(chunk * PIECE, (chunk + 1) * PIECE)
            dst_ref[keeper, rows, :] = part
            dst_ref[keeper + NX, rows, :] = part


def to_rows_kernel(slot_ref, src_ref, dst_ref, sems):
    pairs = []
    for j in range(8):
        slot = slot_ref[0, j]
        keeper = (slot % 2) * 2 * NX + slot // 2
        for half in range(2):
            start = (j % 2) * BLOCK + half * HALF
            pairs.append((src_ref.at[keeper + half * NX], dst_ref.at[j // 2, :, pl.ds(start, HALF)]))
    run_copies(pairs, sems)


def update_kernel(
    side_ref,
    pieces_ref,
    left_ref,
    corner_ref,
    right_ref,
    out_ref,
    g_ref,
    sum_ref,
    g_held,
    t_held,
    out_held,
    sems,
):
    tile = 256
    terms = pieces_ref[:, PIECE_ROWS:, :].astype(jnp.float32)
    sums = terms[:, 0, :] + terms[:, 1, :] + terms[:, 2, :]
    sum_ref[...] = jnp.sum(sums, axis=0, keepdims=True)[:, :1]
    for piece in range(NX * NY):
        for chunk in range(8):
            g_held[piece * PIECE : (piece + 1) * PIECE, chunk * 128 : (chunk + 1) * 128] = pieces_ref[
                piece, chunk * PIECE : (chunk + 1) * PIECE, :
            ]
    copies = [pltpu.make_async_copy(g_held, g_ref, sems.at[4])]
    copies[0].start()
    for i in range(BLOCK // tile):
        rows = slice(i * tile, (i + 1) * tile)
        t_held[rows, :] = lax.dot_general(
            g_held[rows, :], right_ref[...], (((1,), (1,)), ((), ())), preferred_element_type=jnp.float32
        ).astype(jnp.bfloat16)
    per_tile = tile // PIECE
    side = side_ref[0]
    own = pl.multiple_of(side * HALF, HALF)
    other = pl.multiple_of((1 - side) * HALF, HALF)
    t_own = t_held.at[pl.ds(own, HALF)]
    t_other = t_held.at[pl.ds(other, HALF)]
    for i in range(BLOCK // tile):
        part, inner = i // 2, i % 2
        rows = slice(inner * tile, (inner + 1) * tile)
        if part == 0:
            product = jnp.dot(left_ref[rows, :], t_held[...], preferred_element_type=jnp.float32)
            first = side * (HALF // PIECE) + inner * per_tile
        else:
            cross = left_ref[:, pl.ds(pl.multiple_of(other + inner * tile, tile), tile)]
            product = lax.dot_general(
                cross, t_own[...], (((0,), (0,)), ((), ())), preferred_element_type=jnp.float32
            ) + jnp.dot(corner_ref[rows, :], t_other[...], preferred_element_type=jnp.float32)
            first = (1 - side) * (HALF // PIECE) + inner * per_tile
        held = out_held.at[i * per_tile : (i + 1) * per_tile]
        held[...] = product.astype(jnp.bfloat16).reshape(per_tile, PIECE, HALF)
        copy = pltpu.make_async_copy(held, out_ref.at[pl.ds(first, per_tile)], sems.at[i])
        copy.start()
        copies.append(copy)
    for copy in copies:
        copy.wait()


def per_device(grad, left_stat, right_stat, left_root, right_root, block_slot):
    side = lax.axis_index("y") % 2
    corner = lax.dynamic_slice_in_dim(left_root, side * HALF, HALF, 1)
    other_corner = lax.ppermute(corner, "y", [(i, i ^ 1) for i in range(NY)])
    spread = lax.all_to_all(grad.reshape(NX, PIECE, 2 * BLOCK), "x", 0, 0)
    local_sum = jnp.sum(jnp.square(grad.astype(jnp.float32)))
    group_sum = add_partner(add_partner(local_sum.reshape(1, 1), 0), 1)
    spread, other_corner, group_sum = lax.optimization_barrier((spread, other_corner, group_sum))

    send = pl.pallas_call(
        to_keepers_kernel,
        out_shape=jax.ShapeDtypeStruct((NX * NY, PIECE_ROWS + 16, 128), jnp.bfloat16),
        in_specs=[SMEM, VMEM, VMEM],
        out_specs=VMEM,
        compiler_params=pltpu.CompilerParams(vmem_limit_bytes=16 * 1024 * 1024),
    )(block_slot, group_sum, spread)
    pieces = lax.all_to_all(send, ("y", "x"), 0, 0)

    out, g, half_sum = pl.pallas_call(
        update_kernel,
        out_shape=(
            pltpu.HBM((NX * NY, PIECE, HALF), jnp.bfloat16),
            pltpu.HBM((BLOCK, BLOCK), jnp.bfloat16),
            jax.ShapeDtypeStruct((1, 1), jnp.float32),
        ),
        in_specs=[SMEM, VMEM, VMEM, VMEM, VMEM],
        out_specs=(HBM, HBM, VMEM),
        scratch_shapes=[
            pltpu.VMEM((BLOCK, BLOCK), jnp.bfloat16),
            pltpu.VMEM((BLOCK, HALF), jnp.bfloat16),
            pltpu.VMEM((NX * NY, PIECE, HALF), jnp.bfloat16),
            pltpu.SemaphoreType.DMA((5,)),
        ],
        compiler_params=pltpu.CompilerParams(vmem_limit_bytes=32 * 1024 * 1024),
    )(side.reshape(1), pieces, left_root, other_corner, right_root)
    back = lax.all_to_all(out, ("y", "x"), 0, 0)
    sum_squares = add_partner(half_sum, 2)[0, 0]
    grad_rms = jnp.sqrt(sum_squares / (ROWS * COLS) + norm_eps)
    factor = jnp.minimum(1.0, clip_level / grad_rms)
    scale = (1.0 - ema_decay) * factor * factor
    rows_half = lax.dynamic_slice_in_dim(g, side * HALF, HALF, 0)
    cols_half = lax.dynamic_slice_in_dim(g, side * HALF, HALF, 1)
    gram_left = lax.dot_general(
        rows_half, g, (((1,), (1,)), ((), ())), preferred_element_type=jnp.float32
    )
    gram_right = lax.dot_general(
        cols_half, g, (((0,), (0,)), ((), ())), preferred_element_type=jnp.float32
    )
    new_left = ema_decay * left_stat + scale * gram_left
    new_right = ema_decay * right_stat + scale * gram_right
    back, new_left, new_right = lax.optimization_barrier((back, new_left, new_right))
    rows = pl.pallas_call(
        to_rows_kernel,
        out_shape=jax.ShapeDtypeStruct((NX, PIECE, 2 * BLOCK), jnp.bfloat16),
        in_specs=[SMEM, ANY],
        out_specs=ANY,
        scratch_shapes=[pltpu.SemaphoreType.DMA((16,))],
        compiler_params=pltpu.CompilerParams(vmem_limit_bytes=1024 * 1024),
    )(block_slot, back)
    update = lax.all_to_all(rows, "x", 0, 0).reshape(grad.shape)
    update = (update.astype(jnp.float32) * factor).astype(jnp.bfloat16)
    return (new_left, new_right, update, grad_rms)


def solution(mesh):
    grid = Mesh(mesh.devices.reshape(NX, NY, mesh.shape["tp"]), ("x", "y", "tp"))
    split = P(FSDP, "tp")
    return jax.shard_map(
        per_device,
        mesh=grid,
        in_specs=(split, split, split, split, split, P("tp", None)),
        out_specs=(split, split, split, P()),
        check_vma=False,
    )
```

time: 144 us -> 96.7 us (0.67)
  waiting for transfers between devices: 46.7 us -> 8.3 us
  starting transfers between devices: 47.5 us -> 17.2 us
  blocking collectives: 19.6 us -> 48.7 us
  Pallas kernels: 9.55 us -> 5.84 us
  local copies, waits for them, and re-layouts: 3.17 us -> 0.07 us
  between operations: 7.02 us -> 5.16 us
    all_to_all x1 -> x2, blocking collectives: 19.6 us -> 48.7 us  [the longest x1 34 us: per_device(): pieces = lax.all_to_all(send, ('y', 'x'), 0, 0)]
    ppermute x8 -> x4, starting transfers between devices: 32 us -> 8.91 us  [the longest x3 7.25 us: add_partner(): lax.ppermute(value, 'tp', [(i, i ^ 1 << bit) for i in range(8)])]
    ppermute x8 -> x4, waiting for transfers between devices: 25 us -> 5.98 us  [the longest x3 3.58 us: add_partner(): lax.ppermute(value, 'tp', [(i, i ^ 1 << bit) for i in range(8)])]
    all_to_all x1, waiting for transfers between devices: 16.2 us -> 0.74 us  [per_device(): back = lax.all_to_all(out, ('y', 'x'), 0, 0)]
    all_to_all x2 -> x1, starting transfers between devices: 9.01 us -> 4.52 us  [per_device(): spread = lax.all_to_all(grad.reshape(NX, PIECE, 2 * BLOCK), 'x', 0, 0)]
    all_to_all x2 -> x1, waiting for transfers between devices: 5.48 us -> 1.59 us  [per_device(): spread = lax.all_to_all(grad.reshape(NX, PIECE, 2 * BLOCK), 'x', 0, 0)]
    unnamed x9 -> x12, local copies, waits for them, and re-layouts: 3.17 us -> 0.03 us
    all_to_all x1, starting transfers between devices: 6.46 us -> 3.8 us  [per_device(): back = lax.all_to_all(out, ('y', 'x'), 0, 0)]
  transfers between devices with their start and end apart: 11 -> 6, of which waited for: 9 -> 6; matrix products, arithmetic and copies ran while one was open for 7% -> 10% of each run, Pallas kernels for 0% -> 0%
where the time goes in v2:
time: 96.7 us; the launch traced here: 96.2 us
  blocking collectives  48.7 us (50%)
  starting transfers between devices  17.2 us (18%)
  waiting for transfers between devices  8.3 us (9%)
  matrix products  7.31 us (8%)
  Pallas kernels  5.84 us (6%)
  between operations  5.16 us (5%)
  other arithmetic  3.61 us (4%)
    all_to_all x1, blocking collectives, per_device(): pieces = lax.all_to_all(send, ('y', 'x'), 0, 0)  34 us
    all_to_all x1, blocking collectives, per_device(): update = lax.all_to_all(rows, 'x', 0, 0).reshape(grad.shape)  14.7 us
    ppermute x3, starting transfers between devices, add_partner(): lax.ppermute(value, 'tp', [(i, i ^ 1 << bit) for i in range(8)])  7.25 us
    dot_general x1, matrix products, per_device(): lax.dot_general(cols_half, g, (((0,), (0,)), ((), ())), preferred_element...  4.66 us
    all_to_all x1, starting transfers between devices, per_device(): spread = lax.all_to_all(grad.reshape(NX, PIECE, 2 * BLOCK), 'x', 0, 0)  4.52 us
    pallas_call x1, Pallas kernels, per_device(): pl.pallas_call(update_kernel, out_shape=(pltpu.HBM((NX * NY, PIECE, HALF)...  3.97 us
    all_to_all x1, starting transfers between devices, per_device(): back = lax.all_to_all(out, ('y', 'x'), 0, 0)  3.8 us
    ppermute x3, waiting for transfers between devices, add_partner(): lax.ppermute(value, 'tp', [(i, i ^ 1 << bit) for i in range(8)])  3.58 us
  transfers between devices with their start and end apart: 6, of which 6 were waited for; matrix products, arithmetic and copies ran while one was open for 10% of the time, Pallas kernels for 0%

profile of v2, /device:TPU:0, one launch (start us, length us, event | category | flops | bytes accessed | tf_op | source)
XLA Modules:
  0.0 96.2 jit_solution(6911868618114006543)
XLA Ops:
  0.7 4.5 %all-to-all-start = ((bf16[4,64,2048]{2,1,0:T(8,128)(2,1)}), bf16[4,64,2048]{2,1,0:T(8,128)(2,1)S(1)}, u32[]{:S(2)}, u32[]{:S(2)}) async-start(bf16[4,64,2048]{2,1,0:T(8,128)(2,1)} %bitcast.7), calls=%async_computation | async-start | bytes 2097152 | tf_op jit(solution)/shard_map/all_to_all | solution.py:133
  5.2 1.7 %collective-permute-start = (bf16[512,512]{1,0:T(8,128)(2,1)S(1)}, bf16[512,512]{1,0:T(8,128)(2,1)S(1)}, u32[]{:S(2)}, u32[]{:S(2)}) collective-permute-start(bf16[512,512]{1,0:T(8,128)(2,1)S(1)} %constant_dynamic-slice_fusion), channel_id=1, source_target_pairs={{0,8},{8,0},{16,24},{24,16},{1,9},{9,1},{17,25},{25,17},{2,10},{10... | collective-permute-start | bytes 1572872 | tf_op jit(solution)/shard_map/ppermute | solution.py:132
  6.9 2.4 %multiply_reduce_fusion = f32[]{:T(128)} fusion(bf16[256,2048]{1,0:T(8,128)(2,1)} %param.6), kind=kLoop, calls=%fused_computation.3 | loop fusion | flops 1572863 | bytes 1048580 | tf_op jit(solution)/shard_map/reduce_sum | solution.py:134
  9.2 1.4 %collective-permute-done.1 = f32[1,1]{1,0:T(1,128)} collective-permute-done((f32[1,1]{1,0:T(1,128)}, f32[1,1]{1,0:T(1,128)}, u32[]{:S(2)}, u32[]{:S(2)}) %collective-permute-start.1) | collective-permute-done | bytes 36 | tf_op jit(solution)/shard_map/ppermute | solution.py:30
  11.9 3.3 %collective-permute-start.2 = (f32[1,1]{1,0:T(1,128)}, f32[1,1]{1,0:T(1,128)}, u32[]{:S(2)}, u32[]{:S(2)}) collective-permute-start(f32[1,1]{1,0:T(1,128)} %add.30), channel_id=1, source_target_pairs={{0,2},{1,3},{2,0},{3,1},{4,6},{5,7},{6,4},{7,5},{8,10},{9,11},{10,... | collective-permute-start | bytes 20 | tf_op jit(solution)/shard_map/ppermute | solution.py:30
  15.2 0.4 collective-permute-done.2
  16.3 2.4 %collective-permute-done.corner_ref = bf16[512,512]{1,0:T(8,128)(2,1)S(1)} collective-permute-done((bf16[512,512]{1,0:T(8,128)(2,1)S(1)}, bf16[512,512]{1,0:T(8,128)(2,1)S(1)}, u32[]{:S(2)}, u32[]{:S(2)}) %collective-permute-start) | collective-permute-done | bytes 524320 | tf_op jit(solution)/shard_map/ppermute | solution.py:132
  18.7 1.6 %all-to-all-done.src_ref = bf16[4,64,2048]{2,1,0:T(8,128)(2,1)S(1)} async-done(((bf16[4,64,2048]{2,1,0:T(8,128)(2,1)}), bf16[4,64,2048]{2,1,0:T(8,128)(2,1)S(1)}, u32[]{:S(2)}, u32[]{:S(2)}) %all-to-all-start) | async-done | bytes 1048608 | tf_op jit(solution)/shard_map/all_to_all | solution.py:133
  20.3 0.9 shard_map.93
  21.2 0.0 copy-start.1
  21.2 34.0 %all_to_all.20.pieces_ref = bf16[16,528,128]{2,1,0:T(8,128)(2,1)S(1)} all-to-all(bf16[16,528,128]{2,1,0:T(8,128)(2,1)S(1)} %shard_map.93), channel_id=1, replica_groups=mesh['x'=4,'y'=4,'tp'=8] {'y','x'}, dimensions={0} | all-to-all | bytes 4325376 | tf_op jit(solution)/shard_map/all_to_all | solution.py:145
  55.3 4.0 %shard_map.94 = (bf16[16,64,512]{2,1,0:T(8,128)(2,1)}, bf16[1024,1024]{1,0:T(8,128)(2,1)}, f32[1,1]{1,0:T(1,128)}) custom-call(s32[1]{0:T(128)} %bitcast.side_ref, bf16[16,528,128]{2,1,0:T(8,128)(2,1)S(1)} %all_to_all.20.pieces_ref, bf16[512,1024]{1,0:T(8,128)(2,1)S(1)} %copy-done, bf16[512,512]{1,0:T(8,128)(2,1)S(1)} %collective-permute-done.corner_ref, ...), custom_call_target="tpu_custom_call" | custom-call | tf_op jit(solution)/shard_map/pallas_call | solution.py:147
  59.3 0.0 copy-start.3
  59.3 3.8 %all-to-all-start.2 = ((bf16[16,64,512]{2,1,0:T(8,128)(2,1)}), bf16[16,64,512]{2,1,0:T(8,128)(2,1)S(1)}, u32[]{:S(2)}, u32[]{:S(2)}) async-start(bf16[16,64,512]{2,1,0:T(8,128)(2,1)} %get-tuple-element.16), calls=%async_computation.2 | async-start | bytes 2097152 | tf_op jit(solution)/shard_map/all_to_all | solution.py:164
  63.1 4.0 %collective-permute-start.3 = (f32[1,1]{1,0:T(1,128)}, f32[1,1]{1,0:T(1,128)}, u32[]{:S(2)}, u32[]{:S(2)}) collective-permute-start(f32[1,1]{1,0:T(1,128)} %get-tuple-element.17), channel_id=1, source_target_pairs={{0,4},{1,5},{2,6},{3,7},{4,0},{5,1},{6,2},{7,3},{8,12},{9,13},{10,... | collective-permute-start | bytes 20 | tf_op jit(solution)/shard_map/ppermute | solution.py:30
  67.0 1.8 %collective-permute-done.3 = f32[1,1]{1,0:T(1,128)} collective-permute-done((f32[1,1]{1,0:T(1,128)}, f32[1,1]{1,0:T(1,128)}, u32[]{:S(2)}, u32[]{:S(2)}) %collective-permute-start.3) | collective-permute-done | bytes 36 | tf_op jit(solution)/shard_map/ppermute | solution.py:30
  70.2 0.0 copy-start.4
  70.2 0.0 copy-start.5
  70.2 4.7 %multiply_add_fusion = f32[512,1024]{1,0:T(8,128)} fusion(f32[512,1024]{1,0:T(8,128)S(1)} %copy-done.3, bf16[1024,1024]{1,0:T(8,128)(2,1)} %get-tuple-element.18, s32[]{:T(128)S(6)} %select_n.13, f32[]{:T(128)S(6)} %mul.33), kind=kOutput, calls=%fused_computation.1 | convolution fusion | flops 1075314688 | bytes 7340040 | tf_op jit(solution)/shard_map/dot_general | solution.py:174
  74.9 2.7 %multiply_add_fusion.1 = f32[512,1024]{1,0:T(8,128)} fusion(f32[512,1024]{1,0:T(8,128)S(1)} %copy-done.5, bf16[1024,1024]{1,0:T(8,128)(2,1)S(1)} %copy-done.4, s32[]{:T(128)S(6)} %select_n.13, f32[]{:T(128)S(6)} %mul.33), kind=kOutput, calls=%fused_computation.2 | convolution fusion | flops 1075314688 | bytes 7340040 | tf_op jit(solution)/shard_map/dot_general | solution.py:171
  77.5 0.7 all-to-all-done.2.src_ref
  78.3 0.9 shard_map.95
  79.2 14.7 %all_to_all.21 = bf16[4,64,2048]{2,1,0:T(8,128)(2,1)S(1)} all-to-all(bf16[4,64,2048]{2,1,0:T(8,128)(2,1)S(1)} %shard_map.95), channel_id=1, replica_groups=mesh['x'=4,'y'=4,'tp'=8] {'x'}, dimensions={0} | all-to-all | bytes 2097152 | tf_op jit(solution)/shard_map/all_to_all | solution.py:188
  93.9 1.2 %multiply_convert_fusion = bf16[4,64,2048]{2,1,0:T(8,128)(2,1)} fusion(bf16[4,64,2048]{2,1,0:T(8,128)(2,1)S(1)} %all_to_all.21, f32[]{:T(128)S(6)} %min_shard_map.3), kind=kLoop, calls=%fused_computation | loop fusion | flops 1572864 | bytes 2097156 | tf_op jit(solution)/shard_map/convert_element_type | solution.py:189
  (10 shorter events, 0.1 us)
Async XLA Ops:
  0.6 4.5 %copy-start = (bf16[512,1024]{1,0:T(8,128)(2,1)S(1)}, bf16[512,1024]{1,0:T(8,128)(2,1)}, u32[]{:S(2)}) copy-start(bf16[512,1024]{1,0:T(8,128)(2,1)} %left_ref.1) | copy-start | bytes 3145732
  0.6 19.6 %copy-start.2 = (s32[1,8]{1,0:T(1,128)S(1)}, s32[1,8]{1,0:T(1,128)}, u32[]{:S(2)}) copy-start(s32[1,8]{1,0:T(1,128)} %slot_ref.3) | copy-start | bytes 100
  0.7 19.6 %all-to-all-start = ((bf16[4,64,2048]{2,1,0:T(8,128)(2,1)}), bf16[4,64,2048]{2,1,0:T(8,128)(2,1)S(1)}, u32[]{:S(2)}, u32[]{:S(2)}) async-start(bf16[4,64,2048]{2,1,0:T(8,128)(2,1)} %bitcast.7), calls=%async_computation | async-start | bytes 2097152 | tf_op jit(solution)/shard_map/all_to_all | solution.py:133
  5.2 13.5 %collective-permute-start = (bf16[512,512]{1,0:T(8,128)(2,1)S(1)}, bf16[512,512]{1,0:T(8,128)(2,1)S(1)}, u32[]{:S(2)}, u32[]{:S(2)}) collective-permute-start(bf16[512,512]{1,0:T(8,128)(2,1)S(1)} %constant_dynamic-slice_fusion), channel_id=1, source_target_pairs={{0,8},{8,0},{16,24},{24,16},{1,9},{9,1},{17,25},{25,17},{2,10},{10... | collective-permute-start | bytes 1572872 | tf_op jit(solution)/shard_map/ppermute | solution.py:132
  9.2 1.4 %collective-permute-start.1 = (f32[1,1]{1,0:T(1,128)}, f32[1,1]{1,0:T(1,128)}, u32[]{:S(2)}, u32[]{:S(2)}) collective-permute-start(f32[1,1]{1,0:T(1,128)} %bitcast.2), channel_id=1, source_target_pairs={{0,1},{1,0},{2,3},{3,2},{4,5},{5,4},{6,7},{7,6},{8,9},{9,8},{10,11... | collective-permute-start | bytes 20 | tf_op jit(solution)/shard_map/ppermute | solution.py:30
  11.9 3.7 %collective-permute-start.2 = (f32[1,1]{1,0:T(1,128)}, f32[1,1]{1,0:T(1,128)}, u32[]{:S(2)}, u32[]{:S(2)}) collective-permute-start(f32[1,1]{1,0:T(1,128)} %add.30), channel_id=1, source_target_pairs={{0,2},{1,3},{2,0},{3,1},{4,6},{5,7},{6,4},{7,5},{8,10},{9,11},{10,... | collective-permute-start | bytes 20 | tf_op jit(solution)/shard_map/ppermute | solution.py:30
  21.2 34.1 %copy-start.1 = (bf16[512,1024]{1,0:T(8,128)(2,1)S(1)}, bf16[512,1024]{1,0:T(8,128)(2,1)}, u32[]{:S(2)}) copy-start(bf16[512,1024]{1,0:T(8,128)(2,1)} %right_ref.1) | copy-start | bytes 3145732
  59.3 10.9 %copy-start.3 = (f32[512,1024]{1,0:T(8,128)S(1)}, f32[512,1024]{1,0:T(8,128)}, u32[]{:S(2)}) copy-start(f32[512,1024]{1,0:T(8,128)} %param.8) | copy-start | bytes 6291460
  59.3 19.0 %all-to-all-start.2 = ((bf16[16,64,512]{2,1,0:T(8,128)(2,1)}), bf16[16,64,512]{2,1,0:T(8,128)(2,1)S(1)}, u32[]{:S(2)}, u32[]{:S(2)}) async-start(bf16[16,64,512]{2,1,0:T(8,128)(2,1)} %get-tuple-element.16), calls=%async_computation.2 | async-start | bytes 2097152 | tf_op jit(solution)/shard_map/all_to_all | solution.py:164
  63.1 5.7 %collective-permute-start.3 = (f32[1,1]{1,0:T(1,128)}, f32[1,1]{1,0:T(1,128)}, u32[]{:S(2)}, u32[]{:S(2)}) collective-permute-start(f32[1,1]{1,0:T(1,128)} %get-tuple-element.17), channel_id=1, source_target_pairs={{0,4},{1,5},{2,6},{3,7},{4,0},{5,1},{6,2},{7,3},{8,12},{9,13},{10,... | collective-permute-start | bytes 20 | tf_op jit(solution)/shard_map/ppermute | solution.py:30
  70.2 4.7 %copy-start.4 = (bf16[1024,1024]{1,0:T(8,128)(2,1)S(1)}, bf16[1024,1024]{1,0:T(8,128)(2,1)}, u32[]{:S(2)}) copy-start(bf16[1024,1024]{1,0:T(8,128)(2,1)} %get-tuple-element.18) | copy-start | bytes 6291460
  70.2 4.7 %copy-start.5 = (f32[512,1024]{1,0:T(8,128)S(1)}, f32[512,1024]{1,0:T(8,128)}, u32[]{:S(2)}) copy-start(f32[512,1024]{1,0:T(8,128)} %param.7) | copy-start | bytes 6291460

commit v3 on v2

--- a/solution.py
+++ b/solution.py
@@ -13,6 +13,7 @@
 NY = 4
 PIECE = BLOCK // (NX * NY)
 PIECE_ROWS = PIECE * BLOCK // 128
+SUM_SHAPE = (8, 128)
 
 
 ema_decay = 0.9
@@ -26,8 +27,24 @@
 SMEM = pl.BlockSpec(memory_space=pltpu.SMEM)
 
 
-def add_partner(value, bit):
-    return value + lax.ppermute(value, "tp", [(i, i ^ (1 << bit)) for i in range(8)])
+def from_partner(value, bit):
+    return lax.ppermute(value, "tp", [(i, i ^ (1 << bit)) for i in range(8)])
+
+
+def square_sum_kernel(grad_ref, out_ref, held, sems):
+    parts = 4
+    rows = held.shape[0] // parts
+    copies = []
+    for i in range(parts):
+        part = pl.ds(i * rows, rows)
+        copies.append(pltpu.make_async_copy(grad_ref.at[part], held.at[part], sems.at[i]))
+        copies[-1].start()
+    total = jnp.zeros((8, held.shape[1]), jnp.float32)
+    for i in range(parts):
+        copies[i].wait()
+        value = held[i * rows : (i + 1) * rows, :].astype(jnp.float32)
+        total += jnp.sum((value * value).reshape(rows // 8, 8, held.shape[1]), axis=0)
+    out_ref[...] = jnp.broadcast_to(jnp.sum(total).reshape(1, 1), out_ref.shape)
 
 
 def run_copies(pairs, sems):
@@ -38,8 +55,8 @@
         copy.wait()
 
 
-def to_keepers_kernel(slot_ref, sum_ref, src_ref, dst_ref):
-    total = jnp.broadcast_to(sum_ref[...], (16, 128))
+def to_keepers_kernel(slot_ref, own_ref, other_ref, src_ref, dst_ref):
+    total = jnp.broadcast_to(own_ref[:1, :] + other_ref[:1, :], (16, 128))
     high = total.astype(jnp.bfloat16).astype(jnp.float32)
     middle = (total - high).astype(jnp.bfloat16).astype(jnp.float32)
     low = total - high - middle
@@ -77,7 +94,8 @@
     right_ref,
     out_ref,
     g_ref,
-    sum_ref,
+    rms_ref,
+    scale_ref,
     g_held,
     t_held,
     out_held,
@@ -86,19 +104,24 @@
     tile = 256
     terms = pieces_ref[:, PIECE_ROWS:, :].astype(jnp.float32)
     sums = terms[:, 0, :] + terms[:, 1, :] + terms[:, 2, :]
-    sum_ref[...] = jnp.sum(sums, axis=0, keepdims=True)[:, :1]
-    for piece in range(NX * NY):
-        for chunk in range(8):
-            g_held[piece * PIECE : (piece + 1) * PIECE, chunk * 128 : (chunk + 1) * 128] = pieces_ref[
-                piece, chunk * PIECE : (chunk + 1) * PIECE, :
-            ]
-    copies = [pltpu.make_async_copy(g_held, g_ref, sems.at[4])]
-    copies[0].start()
+    sum_squares = jnp.sum(sums, axis=0, keepdims=True)
+    rms = jnp.sqrt(sum_squares / (ROWS * COLS) + norm_eps)
+    factor = jnp.minimum(1.0, clip_level / rms)
+    rms_ref[...] = jnp.broadcast_to(rms, rms_ref.shape)
+    scale_ref[...] = jnp.tile((1.0 - ema_decay) * factor * factor, (8, BLOCK // 128))
+    factor = jnp.tile(factor, (1, HALF // 128))
     for i in range(BLOCK // tile):
+        for piece in range(i * tile // PIECE, (i + 1) * tile // PIECE):
+            for chunk in range(8):
+                g_held[piece * PIECE : (piece + 1) * PIECE, chunk * 128 : (chunk + 1) * 128] = pieces_ref[
+                    piece, chunk * PIECE : (chunk + 1) * PIECE, :
+                ]
         rows = slice(i * tile, (i + 1) * tile)
         t_held[rows, :] = lax.dot_general(
             g_held[rows, :], right_ref[...], (((1,), (1,)), ((), ())), preferred_element_type=jnp.float32
         ).astype(jnp.bfloat16)
+    copies = [pltpu.make_async_copy(g_held, g_ref, sems.at[4])]
+    copies[0].start()
     per_tile = tile // PIECE
     side = side_ref[0]
     own = pl.multiple_of(side * HALF, HALF)
@@ -118,7 +141,7 @@
             ) + jnp.dot(corner_ref[rows, :], t_other[...], preferred_element_type=jnp.float32)
             first = (1 - side) * (HALF // PIECE) + inner * per_tile
         held = out_held.at[i * per_tile : (i + 1) * per_tile]
-        held[...] = product.astype(jnp.bfloat16).reshape(per_tile, PIECE, HALF)
+        held[...] = (product * factor).astype(jnp.bfloat16).reshape(per_tile, PIECE, HALF)
         copy = pltpu.make_async_copy(held, out_ref.at[pl.ds(first, per_tile)], sems.at[i])
         copy.start()
         copies.append(copy)
@@ -131,28 +154,39 @@
     corner = lax.dynamic_slice_in_dim(left_root, side * HALF, HALF, 1)
     other_corner = lax.ppermute(corner, "y", [(i, i ^ 1) for i in range(NY)])
     spread = lax.all_to_all(grad.reshape(NX, PIECE, 2 * BLOCK), "x", 0, 0)
-    local_sum = jnp.sum(jnp.square(grad.astype(jnp.float32)))
-    group_sum = add_partner(add_partner(local_sum.reshape(1, 1), 0), 1)
-    spread, other_corner, group_sum = lax.optimization_barrier((spread, other_corner, group_sum))
+    own_sum = pl.pallas_call(
+        square_sum_kernel,
+        out_shape=jax.ShapeDtypeStruct(SUM_SHAPE, jnp.float32),
+        in_specs=[ANY],
+        out_specs=VMEM,
+        scratch_shapes=[pltpu.VMEM(grad.shape, jnp.bfloat16), pltpu.SemaphoreType.DMA((4,))],
+    )(grad)
+    own_sum += from_partner(own_sum, 0)
+    own_sum += from_partner(own_sum, 1)
+    other_sum = from_partner(own_sum, 2)
+    spread, other_corner, own_sum, other_sum = lax.optimization_barrier(
+        (spread, other_corner, own_sum, other_sum)
+    )
 
     send = pl.pallas_call(
         to_keepers_kernel,
         out_shape=jax.ShapeDtypeStruct((NX * NY, PIECE_ROWS + 16, 128), jnp.bfloat16),
-        in_specs=[SMEM, VMEM, VMEM],
+        in_specs=[SMEM, VMEM, VMEM, VMEM],
         out_specs=VMEM,
         compiler_params=pltpu.CompilerParams(vmem_limit_bytes=16 * 1024 * 1024),
-    )(block_slot, group_sum, spread)
+    )(block_slot, own_sum, other_sum, spread)
     pieces = lax.all_to_all(send, ("y", "x"), 0, 0)
 
-    out, g, half_sum = pl.pallas_call(
+    out, g, rms, scale = pl.pallas_call(
         update_kernel,
         out_shape=(
             pltpu.HBM((NX * NY, PIECE, HALF), jnp.bfloat16),
             pltpu.HBM((BLOCK, BLOCK), jnp.bfloat16),
-            jax.ShapeDtypeStruct((1, 1), jnp.float32),
+            jax.ShapeDtypeStruct(SUM_SHAPE, jnp.float32),
+            jax.ShapeDtypeStruct((8, BLOCK), jnp.float32),
         ),
         in_specs=[SMEM, VMEM, VMEM, VMEM, VMEM],
-        out_specs=(HBM, HBM, VMEM),
+        out_specs=(HBM, HBM, VMEM, VMEM),
         scratch_shapes=[
             pltpu.VMEM((BLOCK, BLOCK), jnp.bfloat16),
             pltpu.VMEM((BLOCK, HALF), jnp.bfloat16),
@@ -162,10 +196,7 @@
         compiler_params=pltpu.CompilerParams(vmem_limit_bytes=32 * 1024 * 1024),
     )(side.reshape(1), pieces, left_root, other_corner, right_root)
     back = lax.all_to_all(out, ("y", "x"), 0, 0)
-    sum_squares = add_partner(half_sum, 2)[0, 0]
-    grad_rms = jnp.sqrt(sum_squares / (ROWS * COLS) + norm_eps)
-    factor = jnp.minimum(1.0, clip_level / grad_rms)
-    scale = (1.0 - ema_decay) * factor * factor
+    scale = scale[:1, :]
     rows_half = lax.dynamic_slice_in_dim(g, side * HALF, HALF, 0)
     cols_half = lax.dynamic_slice_in_dim(g, side * HALF, HALF, 1)
     gram_left = lax.dot_general(
@@ -176,7 +207,8 @@
     )
     new_left = ema_decay * left_stat + scale * gram_left
     new_right = ema_decay * right_stat + scale * gram_right
-    back, new_left, new_right = lax.optimization_barrier((back, new_left, new_right))
+    grad_rms = rms[0, 0]
+    back, new_left, new_right, grad_rms = lax.optimization_barrier((back, new_left, new_right, grad_rms))
     rows = pl.pallas_call(
         to_rows_kernel,
         out_shape=jax.ShapeDtypeStruct((NX, PIECE, 2 * BLOCK), jnp.bfloat16),
@@ -186,7 +218,6 @@
         compiler_params=pltpu.CompilerParams(vmem_limit_bytes=1024 * 1024),
     )(block_slot, back)
     update = lax.all_to_all(rows, "x", 0, 0).reshape(grad.shape)
-    update = (update.astype(jnp.float32) * factor).astype(jnp.bfloat16)
     return (new_left, new_right, update, grad_rms)
 
 

time: 96.7 us -> 95.4 us (0.987)
  between operations: 5.16 us -> 0.74 us
  waiting for transfers between devices: 8.3 us -> 12.2 us
  other arithmetic: 3.61 us -> 0.69 us
  local copies, waits for them, and re-layouts: 0.07 us -> 1.55 us
  starting transfers between devices: 17.2 us -> 15.9 us
  Pallas kernels: 5.84 us -> 6.93 us
  blocking collectives: 48.7 us -> 49.7 us
    all_to_all x1, waiting for transfers between devices: 0.74 us -> 7.4 us  [per_device(): back = lax.all_to_all(out, ('y', 'x'), 0, 0)]
    ppermute x1, waiting for transfers between devices: 2.4 us -> 0.01 us  [per_device(): other_corner = lax.ppermute(corner, 'y', [(i, i ^ 1) for i in range(NY)])]
    reduce_sum x1 -> x0, other arithmetic: 2.37 us -> none  [per_device(): local_sum = jnp.sum(jnp.square(grad.astype(jnp.float32)))]
    pallas_call x0 -> x1, Pallas kernels: none -> 1.96 us  [per_device(): pl.pallas_call(square_sum_kernel, out_shape=jax.ShapeDtypeStruct(SUM_SHAP...]
    all_to_all x1, blocking collectives: 34 us -> 35.8 us  [per_device(): pieces = lax.all_to_all(send, ('y', 'x'), 0, 0)]
    all_to_all x1, waiting for transfers between devices: 1.59 us -> 0.21 us  [per_device(): spread = lax.all_to_all(grad.reshape(NX, PIECE, 2 * BLOCK), 'x', 0, 0)]
    ppermute x3, starting transfers between devices: 7.25 us -> 5.88 us  [from_partner(): return lax.ppermute(value, 'tp', [(i, i ^ 1 << bit) for i in range(8)])]
    convert_element_type x1 -> x0, other arithmetic: 1.24 us -> none  [per_device(): update = (update.astype(jnp.float32) * factor).astype(jnp.bfloat16)]
  transfers between devices with their start and end apart: 6 -> 6, of which waited for: 6 -> 5; matrix products, arithmetic and copies ran while one was open for 10% -> 9% of each run, Pallas kernels for 0% -> 2%
where the time goes in v3:
time: 95.4 us; the launch traced here: 95 us
  blocking collectives  49.7 us (52%)
  starting transfers between devices  15.9 us (17%)
  waiting for transfers between devices  12.2 us (13%)
  matrix products  7.29 us (8%)
  Pallas kernels  6.93 us (7%)
  local copies, waits for them, and re-layouts  1.55 us (2%)
    all_to_all x1, blocking collectives, per_device(): pieces = lax.all_to_all(send, ('y', 'x'), 0, 0)  35.8 us
    all_to_all x1, blocking collectives, per_device(): update = lax.all_to_all(rows, 'x', 0, 0).reshape(grad.shape)  13.8 us
    all_to_all x1, waiting for transfers between devices, per_device(): back = lax.all_to_all(out, ('y', 'x'), 0, 0)  7.4 us
    ppermute x3, starting transfers between devices, from_partner(): return lax.ppermute(value, 'tp', [(i, i ^ 1 << bit) for i in range(8)])  5.88 us
    dot_general x1, matrix products, per_device(): lax.dot_general(cols_half, g, (((0,), (0,)), ((), ())), preferred_element...  4.66 us
    ppermute x3, waiting for transfers between devices, from_partner(): return lax.ppermute(value, 'tp', [(i, i ^ 1 << bit) for i in range(8)])  4.64 us
    all_to_all x1, starting transfers between devices, per_device(): spread = lax.all_to_all(grad.reshape(NX, PIECE, 2 * BLOCK), 'x', 0, 0)  4.52 us
    all_to_all x1, starting transfers between devices, per_device(): back = lax.all_to_all(out, ('y', 'x'), 0, 0)  3.84 us
  transfers between devices with their start and end apart: 6, of which 5 were waited for; matrix products, arithmetic and copies ran while one was open for 9% of the time, Pallas kernels for 2%

profile of v3, /device:TPU:0, one launch (start us, length us, event | category | flops | bytes accessed | tf_op | source)
XLA Modules:
  0.0 95.0 jit_solution(5547471671939860470)
XLA Ops:
  0.7 4.5 %all-to-all-start = ((bf16[4,64,2048]{2,1,0:T(8,128)(2,1)}), bf16[4,64,2048]{2,1,0:T(8,128)(2,1)S(1)}, u32[]{:S(2)}, u32[]{:S(2)}) async-start(bf16[4,64,2048]{2,1,0:T(8,128)(2,1)} %bitcast.7), calls=%async_computation | async-start | bytes 2097152 | tf_op jit(solution)/shard_map/all_to_all | solution.py:156
  5.2 1.7 %collective-permute-start = (bf16[512,512]{1,0:T(8,128)(2,1)S(1)}, bf16[512,512]{1,0:T(8,128)(2,1)S(1)}, u32[]{:S(2)}, u32[]{:S(2)}) collective-permute-start(bf16[512,512]{1,0:T(8,128)(2,1)S(1)} %constant_dynamic-slice_fusion), channel_id=1, source_target_pairs={{0,8},{8,0},{16,24},{24,16},{1,9},{9,1},{17,25},{25,17},{2,10},{10... | collective-permute-start | bytes 1572872 | tf_op jit(solution)/shard_map/ppermute | solution.py:155
  6.9 2.0 %shard_map.93 = f32[8,128]{1,0:T(8,128)} custom-call(bf16[256,2048]{1,0:T(8,128)(2,1)} %grad_ref.1), custom_call_target="tpu_custom_call" | custom-call | tf_op jit(solution)/shard_map/pallas_call | solution.py:157
  8.8 0.1 collective-permute-start.1
  8.9 1.4 %collective-permute-done.1 = f32[8,128]{1,0:T(8,128)S(1)} collective-permute-done((f32[8,128]{1,0:T(8,128)}, f32[8,128]{1,0:T(8,128)S(1)}, u32[]{:S(2)}, u32[]{:S(2)}) %collective-permute-start.1) | collective-permute-done | bytes 4128 | tf_op jit(solution)/shard_map/ppermute | solution.py:31
  10.3 0.7 add.23
  11.0 1.9 %collective-permute-start.2 = (f32[8,128]{1,0:T(8,128)S(1)}, f32[8,128]{1,0:T(8,128)S(1)}, u32[]{:S(2)}, u32[]{:S(2)}) collective-permute-start(f32[8,128]{1,0:T(8,128)S(1)} %add.23), channel_id=1, source_target_pairs={{0,2},{1,3},{2,0},{3,1},{4,6},{5,7},{6,4},{7,5},{8,10},{9,11},{10,... | collective-permute-start | bytes 12296 | tf_op jit(solution)/shard_map/ppermute | solution.py:31
  12.9 1.7 %collective-permute-done.2 = f32[8,128]{1,0:T(8,128)S(1)} collective-permute-done((f32[8,128]{1,0:T(8,128)S(1)}, f32[8,128]{1,0:T(8,128)S(1)}, u32[]{:S(2)}, u32[]{:S(2)}) %collective-permute-start.2) | collective-permute-done | bytes 4128 | tf_op jit(solution)/shard_map/ppermute | solution.py:31
  14.6 3.9 %collective-permute-start.3 = (f32[8,128]{1,0:T(8,128)S(1)}, f32[8,128]{1,0:T(8,128)S(1)}, u32[]{:S(2)}, u32[]{:S(2)}) collective-permute-start(f32[8,128]{1,0:T(8,128)S(1)} %add.24.own_ref), channel_id=1, source_target_pairs={{0,4},{1,5},{2,6},{3,7},{4,0},{5,1},{6,2},{7,3},{8,12},{9,13},{10,... | collective-permute-start | bytes 12296 | tf_op jit(solution)/shard_map/ppermute | solution.py:31
  18.5 1.6 %collective-permute-done.3.other_ref = f32[8,128]{1,0:T(8,128)S(1)} collective-permute-done((f32[8,128]{1,0:T(8,128)S(1)}, f32[8,128]{1,0:T(8,128)S(1)}, u32[]{:S(2)}, u32[]{:S(2)}) %collective-permute-start.3) | collective-permute-done | bytes 4128 | tf_op jit(solution)/shard_map/ppermute | solution.py:31
  20.1 0.2 all-to-all-done.src_ref
  20.3 0.8 shard_map.94
  21.1 0.0 copy-start.1
  21.1 35.8 %all_to_all.20.pieces_ref = bf16[16,528,128]{2,1,0:T(8,128)(2,1)S(1)} all-to-all(bf16[16,528,128]{2,1,0:T(8,128)(2,1)S(1)} %shard_map.94), channel_id=1, replica_groups=mesh['x'=4,'y'=4,'tp'=8] {'y','x'}, dimensions={0} | all-to-all | bytes 4325376 | tf_op jit(solution)/shard_map/all_to_all | solution.py:178
  57.0 3.2 %shard_map.95 = (bf16[16,64,512]{2,1,0:T(8,128)(2,1)}, bf16[1024,1024]{1,0:T(8,128)(2,1)}, f32[8,128]{1,0:T(8,128)S(1)}, f32[8,1024]{1,0:T(8,128)S(1)}) custom-call(s32[1]{0:T(128)} %bitcast.side_ref, bf16[16,528,128]{2,1,0:T(8,128)(2,1)S(1)} %all_to_all.20.pieces_ref, bf16[512,1024]{1,0:T(8,128)(2,1)S(1)} %copy-done, ...), custom_call_target="tpu_custom_call" | custom-call | tf_op jit(solution)/shard_map/pallas_call | solution.py:180
  60.2 0.0 copy-start.3
  60.2 3.8 %all-to-all-start.2 = ((bf16[16,64,512]{2,1,0:T(8,128)(2,1)}), bf16[16,64,512]{2,1,0:T(8,128)(2,1)S(1)}, u32[]{:S(2)}, u32[]{:S(2)}) async-start(bf16[16,64,512]{2,1,0:T(8,128)(2,1)} %get-tuple-element.20), calls=%async_computation.2 | async-start | bytes 2097152 | tf_op jit(solution)/shard_map/all_to_all | solution.py:198
  64.1 0.5 slice.7
  64.6 4.7 %multiply_add_fusion = f32[512,1024]{1,0:T(8,128)} fusion(f32[512,1024]{1,0:T(8,128)S(1)} %copy-done.3, bf16[1024,1024]{1,0:T(8,128)(2,1)} %get-tuple-element.22, s32[]{:T(128)S(6)} %select_n.13, f32[1024]{0:T(1024)S(1)} %bitcast.9), kind=kOutput, calls=%fused_computation | convolution fusion | flops 1075314688 | bytes 7344132 | tf_op jit(solution)/shard_map/dot_general | solution.py:205
  69.3 2.6 %multiply_add_fusion.1 = f32[512,1024]{1,0:T(8,128)} fusion(f32[512,1024]{1,0:T(8,128)S(1)} %copy-done.5, bf16[1024,1024]{1,0:T(8,128)(2,1)S(1)} %copy-done.4, s32[]{:T(128)S(6)} %select_n.13, f32[1024]{0:T(1024)S(1)} %bitcast.10), kind=kOutput, calls=%fused_computation.1 | convolution fusion | flops 1075314688 | bytes 7344132 | tf_op jit(solution)/shard_map/dot_general | solution.py:202
  71.9 7.4 %all-to-all-done.2.src_ref = bf16[16,64,512]{2,1,0:T(8,128)(2,1)S(1)} async-done(((bf16[16,64,512]{2,1,0:T(8,128)(2,1)}), bf16[16,64,512]{2,1,0:T(8,128)(2,1)S(1)}, u32[]{:S(2)}, u32[]{:S(2)}) %all-to-all-start.2) | async-done | bytes 1048608 | tf_op jit(solution)/shard_map/all_to_all | solution.py:198
  79.3 0.9 shard_map.96
  80.2 13.8 %all_to_all.21 = bf16[4,64,2048]{2,1,0:T(8,128)(2,1)S(1)} all-to-all(bf16[4,64,2048]{2,1,0:T(8,128)(2,1)S(1)} %shard_map.96), channel_id=1, replica_groups=mesh['x'=4,'y'=4,'tp'=8] {'x'}, dimensions={0} | all-to-all | bytes 2097152 | tf_op jit(solution)/shard_map/all_to_all | solution.py:220
  94.0 1.0 %copy.11 = bf16[256,2048]{1,0:T(8,128)(2,1)} copy(bf16[256,2048]{1,0:T(8,128)(2,1)S(1)} %bitcast.8) | data formatting | bytes 2097152
  (14 shorter events, 0.1 us)
Async XLA Ops:
  0.6 4.5 %copy-start = (bf16[512,1024]{1,0:T(8,128)(2,1)S(1)}, bf16[512,1024]{1,0:T(8,128)(2,1)}, u32[]{:S(2)}) copy-start(bf16[512,1024]{1,0:T(8,128)(2,1)} %left_ref.1) | copy-start | bytes 3145732
  0.6 19.6 %copy-start.2 = (s32[1,8]{1,0:T(1,128)S(1)}, s32[1,8]{1,0:T(1,128)}, u32[]{:S(2)}) copy-start(s32[1,8]{1,0:T(1,128)} %slot_ref.3) | copy-start | bytes 100
  0.7 19.6 %all-to-all-start = ((bf16[4,64,2048]{2,1,0:T(8,128)(2,1)}), bf16[4,64,2048]{2,1,0:T(8,128)(2,1)S(1)}, u32[]{:S(2)}, u32[]{:S(2)}) async-start(bf16[4,64,2048]{2,1,0:T(8,128)(2,1)} %bitcast.7), calls=%async_computation | async-start | bytes 2097152 | tf_op jit(solution)/shard_map/all_to_all | solution.py:156
  5.2 14.8 %collective-permute-start = (bf16[512,512]{1,0:T(8,128)(2,1)S(1)}, bf16[512,512]{1,0:T(8,128)(2,1)S(1)}, u32[]{:S(2)}, u32[]{:S(2)}) collective-permute-start(bf16[512,512]{1,0:T(8,128)(2,1)S(1)} %constant_dynamic-slice_fusion), channel_id=1, source_target_pairs={{0,8},{8,0},{16,24},{24,16},{1,9},{9,1},{17,25},{25,17},{2,10},{10... | collective-permute-start | bytes 1572872 | tf_op jit(solution)/shard_map/ppermute | solution.py:155
  8.8 1.5 %collective-permute-start.1 = (f32[8,128]{1,0:T(8,128)}, f32[8,128]{1,0:T(8,128)S(1)}, u32[]{:S(2)}, u32[]{:S(2)}) collective-permute-start(f32[8,128]{1,0:T(8,128)} %shard_map.93), channel_id=1, source_target_pairs={{0,1},{1,0},{2,3},{3,2},{4,5},{5,4},{6,7},{7,6},{8,9},{9,8},{10,11... | collective-permute-start | bytes 12296 | tf_op jit(solution)/shard_map/ppermute | solution.py:31
  11.0 3.6 %collective-permute-start.2 = (f32[8,128]{1,0:T(8,128)S(1)}, f32[8,128]{1,0:T(8,128)S(1)}, u32[]{:S(2)}, u32[]{:S(2)}) collective-permute-start(f32[8,128]{1,0:T(8,128)S(1)} %add.23), channel_id=1, source_target_pairs={{0,2},{1,3},{2,0},{3,1},{4,6},{5,7},{6,4},{7,5},{8,10},{9,11},{10,... | collective-permute-start | bytes 12296 | tf_op jit(solution)/shard_map/ppermute | solution.py:31
  14.6 5.5 %collective-permute-start.3 = (f32[8,128]{1,0:T(8,128)S(1)}, f32[8,128]{1,0:T(8,128)S(1)}, u32[]{:S(2)}, u32[]{:S(2)}) collective-permute-start(f32[8,128]{1,0:T(8,128)S(1)} %add.24.own_ref), channel_id=1, source_target_pairs={{0,4},{1,5},{2,6},{3,7},{4,0},{5,1},{6,2},{7,3},{8,12},{9,13},{10,... | collective-permute-start | bytes 12296 | tf_op jit(solution)/shard_map/ppermute | solution.py:31
  21.1 35.9 %copy-start.1 = (bf16[512,1024]{1,0:T(8,128)(2,1)S(1)}, bf16[512,1024]{1,0:T(8,128)(2,1)}, u32[]{:S(2)}) copy-start(bf16[512,1024]{1,0:T(8,128)(2,1)} %right_ref.1) | copy-start | bytes 3145732
  60.2 4.4 %copy-start.3 = (f32[512,1024]{1,0:T(8,128)S(1)}, f32[512,1024]{1,0:T(8,128)}, u32[]{:S(2)}) copy-start(f32[512,1024]{1,0:T(8,128)} %param.8) | copy-start | bytes 6291460
  60.2 19.1 %all-to-all-start.2 = ((bf16[16,64,512]{2,1,0:T(8,128)(2,1)}), bf16[16,64,512]{2,1,0:T(8,128)(2,1)S(1)}, u32[]{:S(2)}, u32[]{:S(2)}) async-start(bf16[16,64,512]{2,1,0:T(8,128)(2,1)} %get-tuple-element.20), calls=%async_computation.2 | async-start | bytes 2097152 | tf_op jit(solution)/shard_map/all_to_all | solution.py:198
  64.6 4.7 %copy-start.4 = (bf16[1024,1024]{1,0:T(8,128)(2,1)S(1)}, bf16[1024,1024]{1,0:T(8,128)(2,1)}, u32[]{:S(2)}) copy-start(bf16[1024,1024]{1,0:T(8,128)(2,1)} %get-tuple-element.22) | copy-start | bytes 6291460
  64.6 4.7 %copy-start.5 = (f32[512,1024]{1,0:T(8,128)S(1)}, f32[512,1024]{1,0:T(8,128)}, u32[]{:S(2)}) copy-start(f32[512,1024]{1,0:T(8,128)} %param.7) | copy-start | bytes 6291460

commit v4 on v3

--- a/solution.py
+++ b/solution.py
@@ -45,14 +45,6 @@
         value = held[i * rows : (i + 1) * rows, :].astype(jnp.float32)
         total += jnp.sum((value * value).reshape(rows // 8, 8, held.shape[1]), axis=0)
     out_ref[...] = jnp.broadcast_to(jnp.sum(total).reshape(1, 1), out_ref.shape)
-
-
-def run_copies(pairs, sems):
-    copies = [pltpu.make_async_copy(src, dst, sems.at[i]) for i, (src, dst) in enumerate(pairs)]
-    for copy in copies:
-        copy.start()
-    for copy in copies:
-        copy.wait()
 
 
 def to_keepers_kernel(slot_ref, own_ref, other_ref, src_ref, dst_ref):
@@ -75,15 +67,13 @@
             dst_ref[keeper + NX, rows, :] = part
 
 
-def to_rows_kernel(slot_ref, src_ref, dst_ref, sems):
-    pairs = []
+def to_rows_kernel(slot_ref, src_ref, dst_ref):
     for j in range(8):
         slot = slot_ref[0, j]
         keeper = (slot % 2) * 2 * NX + slot // 2
         for half in range(2):
             start = (j % 2) * BLOCK + half * HALF
-            pairs.append((src_ref.at[keeper + half * NX], dst_ref.at[j // 2, :, pl.ds(start, HALF)]))
-    run_copies(pairs, sems)
+            dst_ref[j // 2, :, start : start + HALF] = src_ref[keeper + half * NX]
 
 
 def update_kernel(
@@ -212,10 +202,9 @@
     rows = pl.pallas_call(
         to_rows_kernel,
         out_shape=jax.ShapeDtypeStruct((NX, PIECE, 2 * BLOCK), jnp.bfloat16),
-        in_specs=[SMEM, ANY],
-        out_specs=ANY,
-        scratch_shapes=[pltpu.SemaphoreType.DMA((16,))],
-        compiler_params=pltpu.CompilerParams(vmem_limit_bytes=1024 * 1024),
+        in_specs=[SMEM, VMEM],
+        out_specs=VMEM,
+        compiler_params=pltpu.CompilerParams(vmem_limit_bytes=8 * 1024 * 1024),
     )(block_slot, back)
     update = lax.all_to_all(rows, "x", 0, 0).reshape(grad.shape)
     return (new_left, new_right, update, grad_rms)

time: 95.4 us -> 95.1 us (level)
  no operation moved by 1% of the time
where the time goes in v4:
time: 95.1 us; the launch traced here: 94.7 us
  blocking collectives  49.7 us (52%)
  starting transfers between devices  15.9 us (17%)
  waiting for transfers between devices  12.2 us (13%)
  matrix products  7.29 us (8%)
  Pallas kernels  6.62 us (7%)
  local copies, waits for them, and re-layouts  1.55 us (2%)
    all_to_all x1, blocking collectives, per_device(): pieces = lax.all_to_all(send, ('y', 'x'), 0, 0)  35.8 us
    all_to_all x1, blocking collectives, per_device(): update = lax.all_to_all(rows, 'x', 0, 0).reshape(grad.shape)  13.8 us
    all_to_all x1, waiting for transfers between devices, per_device(): back = lax.all_to_all(out, ('y', 'x'), 0, 0)  7.4 us
    ppermute x3, starting transfers between devices, from_partner(): return lax.ppermute(value, 'tp', [(i, i ^ 1 << bit) for i in range(8)])  5.88 us
    dot_general x1, matrix products, per_device(): lax.dot_general(cols_half, g, (((0,), (0,)), ((), ())), preferred_element...  4.66 us
    ppermute x3, waiting for transfers between devices, from_partner(): return lax.ppermute(value, 'tp', [(i, i ^ 1 << bit) for i in range(8)])  4.64 us
    all_to_all x1, starting transfers between devices, per_device(): spread = lax.all_to_all(grad.reshape(NX, PIECE, 2 * BLOCK), 'x', 0, 0)  4.52 us
    all_to_all x1, starting transfers between devices, per_device(): back = lax.all_to_all(out, ('y', 'x'), 0, 0)  3.84 us
  transfers between devices with their start and end apart: 6, of which 5 were waited for; matrix products, arithmetic and copies ran while one was open for 9% of the time, Pallas kernels for 2%

profile of v4, /device:TPU:0, one launch (start us, length us, event | category | flops | bytes accessed | tf_op | source)
XLA Modules:
  0.0 94.7 jit_solution(3405114971378919261)
XLA Ops:
  0.7 4.5 %all-to-all-start = ((bf16[4,64,2048]{2,1,0:T(8,128)(2,1)}), bf16[4,64,2048]{2,1,0:T(8,128)(2,1)S(1)}, u32[]{:S(2)}, u32[]{:S(2)}) async-start(bf16[4,64,2048]{2,1,0:T(8,128)(2,1)} %bitcast.7), calls=%async_computation | async-start | bytes 2097152 | tf_op jit(solution)/shard_map/all_to_all | solution.py:146
  5.2 1.7 %collective-permute-start = (bf16[512,512]{1,0:T(8,128)(2,1)S(1)}, bf16[512,512]{1,0:T(8,128)(2,1)S(1)}, u32[]{:S(2)}, u32[]{:S(2)}) collective-permute-start(bf16[512,512]{1,0:T(8,128)(2,1)S(1)} %constant_dynamic-slice_fusion), channel_id=1, source_target_pairs={{0,8},{8,0},{16,24},{24,16},{1,9},{9,1},{17,25},{25,17},{2,10},{10... | collective-permute-start | bytes 1572872 | tf_op jit(solution)/shard_map/ppermute | solution.py:145
  6.9 2.0 %shard_map.93 = f32[8,128]{1,0:T(8,128)} custom-call(bf16[256,2048]{1,0:T(8,128)(2,1)} %grad_ref.1), custom_call_target="tpu_custom_call" | custom-call | tf_op jit(solution)/shard_map/pallas_call | solution.py:147
  8.8 0.1 collective-permute-start.1
  8.9 1.4 %collective-permute-done.1 = f32[8,128]{1,0:T(8,128)S(1)} collective-permute-done((f32[8,128]{1,0:T(8,128)}, f32[8,128]{1,0:T(8,128)S(1)}, u32[]{:S(2)}, u32[]{:S(2)}) %collective-permute-start.1) | collective-permute-done | bytes 4128 | tf_op jit(solution)/shard_map/ppermute | solution.py:31
  10.3 0.7 add.23
  11.0 1.9 %collective-permute-start.2 = (f32[8,128]{1,0:T(8,128)S(1)}, f32[8,128]{1,0:T(8,128)S(1)}, u32[]{:S(2)}, u32[]{:S(2)}) collective-permute-start(f32[8,128]{1,0:T(8,128)S(1)} %add.23), channel_id=1, source_target_pairs={{0,2},{1,3},{2,0},{3,1},{4,6},{5,7},{6,4},{7,5},{8,10},{9,11},{10,... | collective-permute-start | bytes 12296 | tf_op jit(solution)/shard_map/ppermute | solution.py:31
  12.9 1.7 %collective-permute-done.2 = f32[8,128]{1,0:T(8,128)S(1)} collective-permute-done((f32[8,128]{1,0:T(8,128)S(1)}, f32[8,128]{1,0:T(8,128)S(1)}, u32[]{:S(2)}, u32[]{:S(2)}) %collective-permute-start.2) | collective-permute-done | bytes 4128 | tf_op jit(solution)/shard_map/ppermute | solution.py:31
  14.6 3.9 %collective-permute-start.3 = (f32[8,128]{1,0:T(8,128)S(1)}, f32[8,128]{1,0:T(8,128)S(1)}, u32[]{:S(2)}, u32[]{:S(2)}) collective-permute-start(f32[8,128]{1,0:T(8,128)S(1)} %add.24.own_ref), channel_id=1, source_target_pairs={{0,4},{1,5},{2,6},{3,7},{4,0},{5,1},{6,2},{7,3},{8,12},{9,13},{10,... | collective-permute-start | bytes 12296 | tf_op jit(solution)/shard_map/ppermute | solution.py:31
  18.5 1.6 %collective-permute-done.3.other_ref = f32[8,128]{1,0:T(8,128)S(1)} collective-permute-done((f32[8,128]{1,0:T(8,128)S(1)}, f32[8,128]{1,0:T(8,128)S(1)}, u32[]{:S(2)}, u32[]{:S(2)}) %collective-permute-start.3) | collective-permute-done | bytes 4128 | tf_op jit(solution)/shard_map/ppermute | solution.py:31
  20.1 0.2 all-to-all-done.src_ref
  20.3 0.8 shard_map.94
  21.1 0.0 copy-start.1
  21.1 35.8 %all_to_all.20.pieces_ref = bf16[16,528,128]{2,1,0:T(8,128)(2,1)S(1)} all-to-all(bf16[16,528,128]{2,1,0:T(8,128)(2,1)S(1)} %shard_map.94), channel_id=1, replica_groups=mesh['x'=4,'y'=4,'tp'=8] {'y','x'}, dimensions={0} | all-to-all | bytes 4325376 | tf_op jit(solution)/shard_map/all_to_all | solution.py:168
  57.0 3.2 %shard_map.95 = (bf16[16,64,512]{2,1,0:T(8,128)(2,1)}, bf16[1024,1024]{1,0:T(8,128)(2,1)}, f32[8,128]{1,0:T(8,128)S(1)}, f32[8,1024]{1,0:T(8,128)S(1)}) custom-call(s32[1]{0:T(128)} %bitcast.side_ref, bf16[16,528,128]{2,1,0:T(8,128)(2,1)S(1)} %all_to_all.20.pieces_ref, bf16[512,1024]{1,0:T(8,128)(2,1)S(1)} %copy-done, ...), custom_call_target="tpu_custom_call" | custom-call | tf_op jit(solution)/shard_map/pallas_call | solution.py:170
  60.2 0.0 copy-start.3
  60.2 3.8 %all-to-all-start.2 = ((bf16[16,64,512]{2,1,0:T(8,128)(2,1)}), bf16[16,64,512]{2,1,0:T(8,128)(2,1)S(1)}, u32[]{:S(2)}, u32[]{:S(2)}) async-start(bf16[16,64,512]{2,1,0:T(8,128)(2,1)} %get-tuple-element.20), calls=%async_computation.2 | async-start | bytes 2097152 | tf_op jit(solution)/shard_map/all_to_all | solution.py:188
  64.1 0.5 slice.7
  64.6 4.7 %multiply_add_fusion = f32[512,1024]{1,0:T(8,128)} fusion(f32[512,1024]{1,0:T(8,128)S(1)} %copy-done.3, bf16[1024,1024]{1,0:T(8,128)(2,1)} %get-tuple-element.22, s32[]{:T(128)S(6)} %select_n.13, f32[1024]{0:T(1024)S(1)} %bitcast.9), kind=kOutput, calls=%fused_computation | convolution fusion | flops 1075314688 | bytes 7344132 | tf_op jit(solution)/shard_map/dot_general | solution.py:195
  69.3 2.6 %multiply_add_fusion.1 = f32[512,1024]{1,0:T(8,128)} fusion(f32[512,1024]{1,0:T(8,128)S(1)} %copy-done.5, bf16[1024,1024]{1,0:T(8,128)(2,1)S(1)} %copy-done.4, s32[]{:T(128)S(6)} %select_n.13, f32[1024]{0:T(1024)S(1)} %bitcast.10), kind=kOutput, calls=%fused_computation.1 | convolution fusion | flops 1075314688 | bytes 7344132 | tf_op jit(solution)/shard_map/dot_general | solution.py:192
  71.9 7.4 %all-to-all-done.2.src_ref = bf16[16,64,512]{2,1,0:T(8,128)(2,1)S(1)} async-done(((bf16[16,64,512]{2,1,0:T(8,128)(2,1)}), bf16[16,64,512]{2,1,0:T(8,128)(2,1)S(1)}, u32[]{:S(2)}, u32[]{:S(2)}) %all-to-all-start.2) | async-done | bytes 1048608 | tf_op jit(solution)/shard_map/all_to_all | solution.py:188
  79.3 0.6 shard_map.96
  79.9 13.8 %all_to_all.21 = bf16[4,64,2048]{2,1,0:T(8,128)(2,1)S(1)} all-to-all(bf16[4,64,2048]{2,1,0:T(8,128)(2,1)S(1)} %shard_map.96), channel_id=1, replica_groups=mesh['x'=4,'y'=4,'tp'=8] {'x'}, dimensions={0} | all-to-all | bytes 2097152 | tf_op jit(solution)/shard_map/all_to_all | solution.py:209
  93.7 1.0 %copy.11 = bf16[256,2048]{1,0:T(8,128)(2,1)} copy(bf16[256,2048]{1,0:T(8,128)(2,1)S(1)} %bitcast.8) | data formatting | bytes 2097152
  (14 shorter events, 0.1 us)
Async XLA Ops:
  0.6 4.5 %copy-start = (bf16[512,1024]{1,0:T(8,128)(2,1)S(1)}, bf16[512,1024]{1,0:T(8,128)(2,1)}, u32[]{:S(2)}) copy-start(bf16[512,1024]{1,0:T(8,128)(2,1)} %left_ref.1) | copy-start | bytes 3145732
  0.6 19.6 %copy-start.2 = (s32[1,8]{1,0:T(1,128)S(1)}, s32[1,8]{1,0:T(1,128)}, u32[]{:S(2)}) copy-start(s32[1,8]{1,0:T(1,128)} %slot_ref.3) | copy-start | bytes 100
  0.7 19.6 %all-to-all-start = ((bf16[4,64,2048]{2,1,0:T(8,128)(2,1)}), bf16[4,64,2048]{2,1,0:T(8,128)(2,1)S(1)}, u32[]{:S(2)}, u32[]{:S(2)}) async-start(bf16[4,64,2048]{2,1,0:T(8,128)(2,1)} %bitcast.7), calls=%async_computation | async-start | bytes 2097152 | tf_op jit(solution)/shard_map/all_to_all | solution.py:146
  5.2 14.8 %collective-permute-start = (bf16[512,512]{1,0:T(8,128)(2,1)S(1)}, bf16[512,512]{1,0:T(8,128)(2,1)S(1)}, u32[]{:S(2)}, u32[]{:S(2)}) collective-permute-start(bf16[512,512]{1,0:T(8,128)(2,1)S(1)} %constant_dynamic-slice_fusion), channel_id=1, source_target_pairs={{0,8},{8,0},{16,24},{24,16},{1,9},{9,1},{17,25},{25,17},{2,10},{10... | collective-permute-start | bytes 1572872 | tf_op jit(solution)/shard_map/ppermute | solution.py:145
  8.8 1.5 %collective-permute-start.1 = (f32[8,128]{1,0:T(8,128)}, f32[8,128]{1,0:T(8,128)S(1)}, u32[]{:S(2)}, u32[]{:S(2)}) collective-permute-start(f32[8,128]{1,0:T(8,128)} %shard_map.93), channel_id=1, source_target_pairs={{0,1},{1,0},{2,3},{3,2},{4,5},{5,4},{6,7},{7,6},{8,9},{9,8},{10,11... | collective-permute-start | bytes 12296 | tf_op jit(solution)/shard_map/ppermute | solution.py:31
  11.0 3.6 %collective-permute-start.2 = (f32[8,128]{1,0:T(8,128)S(1)}, f32[8,128]{1,0:T(8,128)S(1)}, u32[]{:S(2)}, u32[]{:S(2)}) collective-permute-start(f32[8,128]{1,0:T(8,128)S(1)} %add.23), channel_id=1, source_target_pairs={{0,2},{1,3},{2,0},{3,1},{4,6},{5,7},{6,4},{7,5},{8,10},{9,11},{10,... | collective-permute-start | bytes 12296 | tf_op jit(solution)/shard_map/ppermute | solution.py:31
  14.6 5.5 %collective-permute-start.3 = (f32[8,128]{1,0:T(8,128)S(1)}, f32[8,128]{1,0:T(8,128)S(1)}, u32[]{:S(2)}, u32[]{:S(2)}) collective-permute-start(f32[8,128]{1,0:T(8,128)S(1)} %add.24.own_ref), channel_id=1, source_target_pairs={{0,4},{1,5},{2,6},{3,7},{4,0},{5,1},{6,2},{7,3},{8,12},{9,13},{10,... | collective-permute-start | bytes 12296 | tf_op jit(solution)/shard_map/ppermute | solution.py:31
  21.1 35.9 %copy-start.1 = (bf16[512,1024]{1,0:T(8,128)(2,1)S(1)}, bf16[512,1024]{1,0:T(8,128)(2,1)}, u32[]{:S(2)}) copy-start(bf16[512,1024]{1,0:T(8,128)(2,1)} %right_ref.1) | copy-start | bytes 3145732
  60.2 4.4 %copy-start.3 = (f32[512,1024]{1,0:T(8,128)S(1)}, f32[512,1024]{1,0:T(8,128)}, u32[]{:S(2)}) copy-start(f32[512,1024]{1,0:T(8,128)} %param.8) | copy-start | bytes 6291460
  60.2 19.1 %all-to-all-start.2 = ((bf16[16,64,512]{2,1,0:T(8,128)(2,1)}), bf16[16,64,512]{2,1,0:T(8,128)(2,1)S(1)}, u32[]{:S(2)}, u32[]{:S(2)}) async-start(bf16[16,64,512]{2,1,0:T(8,128)(2,1)} %get-tuple-element.20), calls=%async_computation.2 | async-start | bytes 2097152 | tf_op jit(solution)/shard_map/all_to_all | solution.py:188
  64.6 4.7 %copy-start.4 = (bf16[1024,1024]{1,0:T(8,128)(2,1)S(1)}, bf16[1024,1024]{1,0:T(8,128)(2,1)}, u32[]{:S(2)}) copy-start(bf16[1024,1024]{1,0:T(8,128)(2,1)} %get-tuple-element.22) | copy-start | bytes 6291460
  64.6 4.7 %copy-start.5 = (f32[512,1024]{1,0:T(8,128)S(1)}, f32[512,1024]{1,0:T(8,128)}, u32[]{:S(2)}) copy-start(f32[512,1024]{1,0:T(8,128)} %param.7) | copy-start | bytes 6291460

commit v5 on v4

--- a/solution.py
+++ b/solution.py
@@ -31,19 +31,12 @@
     return lax.ppermute(value, "tp", [(i, i ^ (1 << bit)) for i in range(8)])
 
 
-def square_sum_kernel(grad_ref, out_ref, held, sems):
-    parts = 4
-    rows = held.shape[0] // parts
-    copies = []
-    for i in range(parts):
-        part = pl.ds(i * rows, rows)
-        copies.append(pltpu.make_async_copy(grad_ref.at[part], held.at[part], sems.at[i]))
-        copies[-1].start()
-    total = jnp.zeros((8, held.shape[1]), jnp.float32)
-    for i in range(parts):
-        copies[i].wait()
-        value = held[i * rows : (i + 1) * rows, :].astype(jnp.float32)
-        total += jnp.sum((value * value).reshape(rows // 8, 8, held.shape[1]), axis=0)
+def square_sum_kernel(grad_ref, out_ref):
+    rows = 64
+    total = jnp.zeros((8, grad_ref.shape[1]), jnp.float32)
+    for first in range(0, grad_ref.shape[0], rows):
+        value = grad_ref[first : first + rows, :].astype(jnp.float32)
+        total += jnp.sum((value * value).reshape(rows // 8, 8, grad_ref.shape[1]), axis=0)
     out_ref[...] = jnp.broadcast_to(jnp.sum(total).reshape(1, 1), out_ref.shape)
 
 
@@ -147,9 +140,9 @@
     own_sum = pl.pallas_call(
         square_sum_kernel,
         out_shape=jax.ShapeDtypeStruct(SUM_SHAPE, jnp.float32),
-        in_specs=[ANY],
+        in_specs=[VMEM],
         out_specs=VMEM,
-        scratch_shapes=[pltpu.VMEM(grad.shape, jnp.bfloat16), pltpu.SemaphoreType.DMA((4,))],
+        compiler_params=pltpu.CompilerParams(vmem_limit_bytes=4 * 1024 * 1024),
     )(grad)
     own_sum += from_partner(own_sum, 0)
     own_sum += from_partner(own_sum, 1)

time: 95.1 us -> 93.9 us (0.987)
  Pallas kernels: 6.62 us -> 4.86 us
  waiting for transfers between devices: 12.2 us -> 13.8 us
  blocking collectives: 49.7 us -> 48.6 us
    pallas_call x1, Pallas kernels: 1.96 us -> 0.19 us  [per_device(): pl.pallas_call(square_sum_kernel, out_shape=jax.ShapeDtypeStruct(SUM_SHAP...]
    ppermute x1, waiting for transfers between devices: 0.01 us -> 1.28 us  [per_device(): other_corner = lax.ppermute(corner, 'y', [(i, i ^ 1) for i in range(NY)])]
    all_to_all x1, blocking collectives: 35.8 us -> 34.8 us  [per_device(): pieces = lax.all_to_all(send, ('y', 'x'), 0, 0)]
  transfers between devices with their start and end apart: 6 -> 6, of which waited for: 5 -> 6; matrix products, arithmetic and copies ran while one was open for 9% -> 8% of each run, Pallas kernels for 2% -> 0%
where the time goes in v5:
time: 93.9 us; the launch traced here: 93.6 us
  blocking collectives  48.6 us (52%)
  starting transfers between devices  15.9 us (17%)
  waiting for transfers between devices  13.8 us (15%)
  matrix products  7.32 us (8%)
  Pallas kernels  4.86 us (5%)
  local copies, waits for them, and re-layouts  2.36 us (3%)
    all_to_all x1, blocking collectives, per_device(): pieces = lax.all_to_all(send, ('y', 'x'), 0, 0)  34.8 us
    all_to_all x1, blocking collectives, per_device(): update = lax.all_to_all(rows, 'x', 0, 0).reshape(grad.shape)  13.8 us
    all_to_all x1, waiting for transfers between devices, per_device(): back = lax.all_to_all(out, ('y', 'x'), 0, 0)  7.32 us
    ppermute x3, starting transfers between devices, from_partner(): return lax.ppermute(value, 'tp', [(i, i ^ 1 << bit) for i in range(8)])  5.88 us
    dot_general x1, matrix products, per_device(): lax.dot_general(cols_half, g, (((0,), (0,)), ((), ())), preferred_element...  4.66 us
    all_to_all x1, starting transfers between devices, per_device(): spread = lax.all_to_all(grad.reshape(NX, PIECE, 2 * BLOCK), 'x', 0, 0)  4.52 us
    ppermute x3, waiting for transfers between devices, from_partner(): return lax.ppermute(value, 'tp', [(i, i ^ 1 << bit) for i in range(8)])  4.43 us
    all_to_all x1, starting transfers between devices, per_device(): back = lax.all_to_all(out, ('y', 'x'), 0, 0)  3.8 us
  transfers between devices with their start and end apart: 6, of which 6 were waited for; matrix products, arithmetic and copies ran while one was open for 8% of the time, Pallas kernels for 0%

profile of v5, /device:TPU:0, one launch (start us, length us, event | category | flops | bytes accessed | tf_op | source)
XLA Modules:
  0.0 93.6 jit_solution(14837547636397576100)
XLA Ops:
  0.7 4.5 %all-to-all-start = ((bf16[4,64,2048]{2,1,0:T(8,128)(2,1)}), bf16[4,64,2048]{2,1,0:T(8,128)(2,1)S(1)}, u32[]{:S(2)}, u32[]{:S(2)}) async-start(bf16[4,64,2048]{2,1,0:T(8,128)(2,1)} %bitcast.7), calls=%async_computation | async-start | bytes 2097152 | tf_op jit(solution)/shard_map/all_to_all | solution.py:139
  5.2 1.7 %collective-permute-start = (bf16[512,512]{1,0:T(8,128)(2,1)S(1)}, bf16[512,512]{1,0:T(8,128)(2,1)S(1)}, u32[]{:S(2)}, u32[]{:S(2)}) collective-permute-start(bf16[512,512]{1,0:T(8,128)(2,1)S(1)} %constant_dynamic-slice_fusion), channel_id=1, source_target_pairs={{0,8},{8,0},{16,24},{24,16},{1,9},{9,1},{17,25},{25,17},{2,10},{10... | collective-permute-start | bytes 1572872 | tf_op jit(solution)/shard_map/ppermute | solution.py:138
  6.9 0.2 shard_map.93
  7.1 0.1 collective-permute-start.1
  7.2 1.2 %collective-permute-done.1 = f32[8,128]{1,0:T(8,128)S(1)} collective-permute-done((f32[8,128]{1,0:T(8,128)S(1)}, f32[8,128]{1,0:T(8,128)S(1)}, u32[]{:S(2)}, u32[]{:S(2)}) %collective-permute-start.1) | collective-permute-done | bytes 4128 | tf_op jit(solution)/shard_map/ppermute | solution.py:31
  8.3 1.9 %collective-permute-start.2 = (f32[8,128]{1,0:T(8,128)S(1)}, f32[8,128]{1,0:T(8,128)S(1)}, u32[]{:S(2)}, u32[]{:S(2)}) collective-permute-start(f32[8,128]{1,0:T(8,128)S(1)} %add.23), channel_id=1, source_target_pairs={{0,2},{1,3},{2,0},{3,1},{4,6},{5,7},{6,4},{7,5},{8,10},{9,11},{10,... | collective-permute-start | bytes 12296 | tf_op jit(solution)/shard_map/ppermute | solution.py:31
  10.2 1.7 %collective-permute-done.2 = f32[8,128]{1,0:T(8,128)S(1)} collective-permute-done((f32[8,128]{1,0:T(8,128)S(1)}, f32[8,128]{1,0:T(8,128)S(1)}, u32[]{:S(2)}, u32[]{:S(2)}) %collective-permute-start.2) | collective-permute-done | bytes 4128 | tf_op jit(solution)/shard_map/ppermute | solution.py:31
  11.9 3.9 %collective-permute-start.3 = (f32[8,128]{1,0:T(8,128)S(1)}, f32[8,128]{1,0:T(8,128)S(1)}, u32[]{:S(2)}, u32[]{:S(2)}) collective-permute-start(f32[8,128]{1,0:T(8,128)S(1)} %add.24.own_ref), channel_id=1, source_target_pairs={{0,4},{1,5},{2,6},{3,7},{4,0},{5,1},{6,2},{7,3},{8,12},{9,13},{10,... | collective-permute-start | bytes 12296 | tf_op jit(solution)/shard_map/ppermute | solution.py:31
  15.8 1.6 %collective-permute-done.3.other_ref = f32[8,128]{1,0:T(8,128)S(1)} collective-permute-done((f32[8,128]{1,0:T(8,128)S(1)}, f32[8,128]{1,0:T(8,128)S(1)}, u32[]{:S(2)}, u32[]{:S(2)}) %collective-permute-start.3) | collective-permute-done | bytes 4128 | tf_op jit(solution)/shard_map/ppermute | solution.py:31
  17.4 1.3 %collective-permute-done.corner_ref = bf16[512,512]{1,0:T(8,128)(2,1)S(1)} collective-permute-done((bf16[512,512]{1,0:T(8,128)(2,1)S(1)}, bf16[512,512]{1,0:T(8,128)(2,1)S(1)}, u32[]{:S(2)}, u32[]{:S(2)}) %collective-permute-start) | collective-permute-done | bytes 524320 | tf_op jit(solution)/shard_map/ppermute | solution.py:138
  18.7 0.8 copy-done.3
  19.5 0.8 all-to-all-done.src_ref
  20.3 0.8 shard_map.94
  21.1 34.8 %all_to_all.20.pieces_ref = bf16[16,528,128]{2,1,0:T(8,128)(2,1)S(1)} all-to-all(bf16[16,528,128]{2,1,0:T(8,128)(2,1)S(1)} %shard_map.94), channel_id=1, replica_groups=mesh['x'=4,'y'=4,'tp'=8] {'y','x'}, dimensions={0} | all-to-all | bytes 4325376 | tf_op jit(solution)/shard_map/all_to_all | solution.py:161
  56.0 3.2 %shard_map.95 = (bf16[16,64,512]{2,1,0:T(8,128)(2,1)}, bf16[1024,1024]{1,0:T(8,128)(2,1)}, f32[8,128]{1,0:T(8,128)S(1)}, f32[8,1024]{1,0:T(8,128)S(1)}) custom-call(s32[1]{0:T(128)} %bitcast.side_ref, bf16[16,528,128]{2,1,0:T(8,128)(2,1)S(1)} %all_to_all.20.pieces_ref, bf16[512,1024]{1,0:T(8,128)(2,1)S(1)} %copy-done.1, bf16[512,512]{1,0:T(8,128)(2,1)S(1)} %copy-done.4, ...), custom_call_target="tpu_custom_call" | custom-call | tf_op jit(solution)/shard_map/pallas_call | solution.py:163
  59.2 3.8 %all-to-all-start.2 = ((bf16[16,64,512]{2,1,0:T(8,128)(2,1)}), bf16[16,64,512]{2,1,0:T(8,128)(2,1)S(1)}, u32[]{:S(2)}, u32[]{:S(2)}) async-start(bf16[16,64,512]{2,1,0:T(8,128)(2,1)} %get-tuple-element.20), calls=%async_computation.2 | async-start | bytes 2097152 | tf_op jit(solution)/shard_map/all_to_all | solution.py:181
  63.0 0.5 slice.7
  63.6 0.0 copy-start.8
  63.6 4.7 %multiply_add_fusion = f32[512,1024]{1,0:T(8,128)} fusion(f32[512,1024]{1,0:T(8,128)S(1)} %copy-done.6, bf16[1024,1024]{1,0:T(8,128)(2,1)} %get-tuple-element.22, s32[]{:T(128)S(6)} %select_n.13, f32[1024]{0:T(1024)S(1)} %bitcast.9), kind=kOutput, calls=%fused_computation | convolution fusion | flops 1075314688 | bytes 7344132 | tf_op jit(solution)/shard_map/dot_general | solution.py:188
  68.2 2.7 %multiply_add_fusion.1 = f32[512,1024]{1,0:T(8,128)} fusion(f32[512,1024]{1,0:T(8,128)S(1)} %copy-done.8, bf16[1024,1024]{1,0:T(8,128)(2,1)S(1)} %copy-done.7, s32[]{:T(128)S(6)} %select_n.13, f32[1024]{0:T(1024)S(1)} %bitcast.10), kind=kOutput, calls=%fused_computation.1 | convolution fusion | flops 1075314688 | bytes 7344132 | tf_op jit(solution)/shard_map/dot_general | solution.py:185
  70.9 7.3 %all-to-all-done.2.src_ref = bf16[16,64,512]{2,1,0:T(8,128)(2,1)S(1)} async-done(((bf16[16,64,512]{2,1,0:T(8,128)(2,1)}), bf16[16,64,512]{2,1,0:T(8,128)(2,1)S(1)}, u32[]{:S(2)}, u32[]{:S(2)}) %all-to-all-start.2) | async-done | bytes 1048608 | tf_op jit(solution)/shard_map/all_to_all | solution.py:181
  78.2 0.6 shard_map.96
  78.8 13.8 %all_to_all.21 = bf16[4,64,2048]{2,1,0:T(8,128)(2,1)S(1)} all-to-all(bf16[4,64,2048]{2,1,0:T(8,128)(2,1)S(1)} %shard_map.96), channel_id=1, replica_groups=mesh['x'=4,'y'=4,'tp'=8] {'x'}, dimensions={0} | all-to-all | bytes 2097152 | tf_op jit(solution)/shard_map/all_to_all | solution.py:202
  92.6 1.0 %copy.11 = bf16[256,2048]{1,0:T(8,128)(2,1)} copy(bf16[256,2048]{1,0:T(8,128)(2,1)S(1)} %bitcast.8) | data formatting | bytes 2097152
  (20 shorter events, 0.1 us)
Async XLA Ops:
  0.6 6.2 %copy-start = (bf16[256,2048]{1,0:T(8,128)(2,1)S(1)}, bf16[256,2048]{1,0:T(8,128)(2,1)}, u32[]{:S(2)}) copy-start(bf16[256,2048]{1,0:T(8,128)(2,1)} %grad_ref.1) | copy-start | bytes 3145732
  0.6 4.5 %copy-start.1 = (bf16[512,1024]{1,0:T(8,128)(2,1)S(1)}, bf16[512,1024]{1,0:T(8,128)(2,1)}, u32[]{:S(2)}) copy-start(bf16[512,1024]{1,0:T(8,128)(2,1)} %left_ref.1) | copy-start | bytes 3145732
  0.7 19.6 %copy-start.5 = (s32[1,8]{1,0:T(1,128)S(1)}, s32[1,8]{1,0:T(1,128)}, u32[]{:S(2)}) copy-start(s32[1,8]{1,0:T(1,128)} %slot_ref.3) | copy-start | bytes 100
  0.7 19.6 %all-to-all-start = ((bf16[4,64,2048]{2,1,0:T(8,128)(2,1)}), bf16[4,64,2048]{2,1,0:T(8,128)(2,1)S(1)}, u32[]{:S(2)}, u32[]{:S(2)}) async-start(bf16[4,64,2048]{2,1,0:T(8,128)(2,1)} %bitcast.7), calls=%async_computation | async-start | bytes 2097152 | tf_op jit(solution)/shard_map/all_to_all | solution.py:139
  5.2 13.5 %collective-permute-start = (bf16[512,512]{1,0:T(8,128)(2,1)S(1)}, bf16[512,512]{1,0:T(8,128)(2,1)S(1)}, u32[]{:S(2)}, u32[]{:S(2)}) collective-permute-start(bf16[512,512]{1,0:T(8,128)(2,1)S(1)} %constant_dynamic-slice_fusion), channel_id=1, source_target_pairs={{0,8},{8,0},{16,24},{24,16},{1,9},{9,1},{17,25},{25,17},{2,10},{10... | collective-permute-start | bytes 1572872 | tf_op jit(solution)/shard_map/ppermute | solution.py:138
  7.1 1.2 %collective-permute-start.1 = (f32[8,128]{1,0:T(8,128)S(1)}, f32[8,128]{1,0:T(8,128)S(1)}, u32[]{:S(2)}, u32[]{:S(2)}) collective-permute-start(f32[8,128]{1,0:T(8,128)S(1)} %shard_map.93), channel_id=1, source_target_pairs={{0,1},{1,0},{2,3},{3,2},{4,5},{5,4},{6,7},{7,6},{8,9},{9,8},{10,11... | collective-permute-start | bytes 12296 | tf_op jit(solution)/shard_map/ppermute | solution.py:31
  8.3 3.6 %collective-permute-start.2 = (f32[8,128]{1,0:T(8,128)S(1)}, f32[8,128]{1,0:T(8,128)S(1)}, u32[]{:S(2)}, u32[]{:S(2)}) collective-permute-start(f32[8,128]{1,0:T(8,128)S(1)} %add.23), channel_id=1, source_target_pairs={{0,2},{1,3},{2,0},{3,1},{4,6},{5,7},{6,4},{7,5},{8,10},{9,11},{10,... | collective-permute-start | bytes 12296 | tf_op jit(solution)/shard_map/ppermute | solution.py:31
  11.9 5.5 %collective-permute-start.3 = (f32[8,128]{1,0:T(8,128)S(1)}, f32[8,128]{1,0:T(8,128)S(1)}, u32[]{:S(2)}, u32[]{:S(2)}) collective-permute-start(f32[8,128]{1,0:T(8,128)S(1)} %add.24.own_ref), channel_id=1, source_target_pairs={{0,4},{1,5},{2,6},{3,7},{4,0},{5,1},{6,2},{7,3},{8,12},{9,13},{10,... | collective-permute-start | bytes 12296 | tf_op jit(solution)/shard_map/ppermute | solution.py:31
  18.7 0.8 copy-start.3
  21.1 34.9 %copy-start.2 = (bf16[512,1024]{1,0:T(8,128)(2,1)S(1)}, bf16[512,1024]{1,0:T(8,128)(2,1)}, u32[]{:S(2)}) copy-start(bf16[512,1024]{1,0:T(8,128)(2,1)} %right_ref.1) | copy-start | bytes 3145732
  21.1 34.9 %copy-start.4 = (bf16[512,512]{1,0:T(8,128)(2,1)S(1)}, bf16[512,512]{1,0:T(8,128)(2,1)}, u32[]{:S(2)}) copy-start(bf16[512,512]{1,0:T(8,128)(2,1)} %copy-done.3) | copy-start | bytes 1572868
  59.2 4.3 %copy-start.6 = (f32[512,1024]{1,0:T(8,128)S(1)}, f32[512,1024]{1,0:T(8,128)}, u32[]{:S(2)}) copy-start(f32[512,1024]{1,0:T(8,128)} %param.8) | copy-start | bytes 6291460
  59.2 19.0 %all-to-all-start.2 = ((bf16[16,64,512]{2,1,0:T(8,128)(2,1)}), bf16[16,64,512]{2,1,0:T(8,128)(2,1)S(1)}, u32[]{:S(2)}, u32[]{:S(2)}) async-start(bf16[16,64,512]{2,1,0:T(8,128)(2,1)} %get-tuple-element.20), calls=%async_computation.2 | async-start | bytes 2097152 | tf_op jit(solution)/shard_map/all_to_all | solution.py:181
  63.5 4.7 %copy-start.7 = (bf16[1024,1024]{1,0:T(8,128)(2,1)S(1)}, bf16[1024,1024]{1,0:T(8,128)(2,1)}, u32[]{:S(2)}) copy-start(bf16[1024,1024]{1,0:T(8,128)(2,1)} %get-tuple-element.22) | copy-start | bytes 6291460
  63.6 4.7 %copy-start.8 = (f32[512,1024]{1,0:T(8,128)S(1)}, f32[512,1024]{1,0:T(8,128)}, u32[]{:S(2)}) copy-start(f32[512,1024]{1,0:T(8,128)} %param.7) | copy-start | bytes 6291460
